TPU v7x, 128 devices: a whole 4x4x4 slice. The times are simulated.
128 devices in a mesh: hold: 16 (over y, x_hi, core), bulk: 8 (over z, x_lo).
Axes of the slice: x: 4 (x_hi: 2, x_lo: 2; x = x_hi * 2 + x_lo), y: 4, z: 4, core: 2. Of those that a mesh axis runs over, the one named last changes fastest.
Arguments:
- queries: bfloat16 [2048, 8192], P(('hold', 'bulk')), may hold values from -12 to 12
- out_grad: bfloat16 [2048, 8192], P(('hold', 'bulk')), may hold values from -48 to 48
- attn_out: bfloat16 [2048, 8192], P(('hold', 'bulk')), may hold values from -3 to 3
- log_totals: float32 [2048, 64], P('hold', 'bulk'), may hold values from 11 to 13
- prompt_keys: bfloat16 [16384, 1024], P('hold', 'bulk'), may hold values from -6 to 6
- prompt_values: bfloat16 [16384, 1024], P('hold', 'bulk'), may hold values from -6 to 6
- rollout_keys: bfloat16 [2048, 1024], P('hold', 'bulk'), may hold values from -6 to 6
- rollout_values: bfloat16 [2048, 1024], P('hold', 'bulk'), may hold values from -6 to 6
- rollout_blocks: int32 [8], replicated, may hold values from 1 to 4, 16 in all
Outputs:
- query_grad: bfloat16 [2048, 8192], P(('hold', 'bulk'))
- prompt_key_grad: float32 [16384, 1024], P('hold', 'bulk')
- prompt_value_grad: float32 [16384, 1024], P('hold', 'bulk')
- rollout_key_grad: float32 [2048, 1024], P('hold', 'bulk')
- rollout_value_grad: float32 [2048, 1024], P('hold', 'bulk')
Inputs may be any that keep to these rules, and one draw needn't show every extreme that they name: `rollout_blocks`: the entries sum to 16; the largest is exactly 4.
All inputs are finite; a program needn't handle non-finite values.
Results may differ from a plain program's by a relative error of at most 0.0055.
Values may be sent and summed in bfloat16 or wider, within the bound.
No kernel may reach another device: no remote copies, remote signals or barrier semaphores. Data moves between devices by JAX's collectives and lax.ppermute only.
A program may use at most 128 MiB of HBM per device.

v0:
```python
import jax
import jax.numpy as jnp
from jax import lax
from jax.sharding import PartitionSpec as P

HD = 128
GROUP = 8
BLOCK = 128
PDEV = 1024
ROWS_DEV = 128


def segment_of(positions, ends):
    return jnp.sum((positions[:, None] >= ends[None, :]).astype(jnp.int32), axis=1)


def block_grads(
    query, grad_out, log_total, offset_term, query_rows, keys, values, key_prompt, key_rows, ends
):
    scale = HD ** (-0.5)
    query_seg = segment_of(query_rows, ends)
    key_seg = segment_of(jnp.maximum(key_rows, 0), ends)
    allowed = key_prompt[None, :] | (query_seg[:, None] == key_seg[None, :]) & (
        key_rows[None, :] <= query_rows[:, None]
    )
    scores = jnp.einsum("nkgd,mkd->nkgm", query, keys, preferred_element_type=jnp.float32) * scale
    prob = jnp.where(allowed[:, None, None, :], jnp.exp(scores - log_total[..., None]), 0.0)
    prob_b = prob.astype(jnp.bfloat16)
    value_grad = jnp.einsum("nkgm,nkgd->mkd", prob_b, grad_out, preferred_element_type=jnp.float32)
    dprob = jnp.einsum("nkgd,mkd->nkgm", grad_out, values, preferred_element_type=jnp.float32)
    dscore = (prob * (dprob - offset_term[..., None])).astype(jnp.bfloat16)
    query_grad = (
        jnp.einsum("nkgm,mkd->nkgd", dscore, keys, preferred_element_type=jnp.float32) * scale
    )
    key_grad = (
        jnp.einsum("nkgm,nkgd->mkd", dscore, query, preferred_element_type=jnp.float32) * scale
    )
    return (query_grad, key_grad, value_grad)


def shards(
    queries,
    out_grad,
    attn_out,
    log_totals,
    prompt_keys,
    prompt_values,
    rollout_keys,
    rollout_values,
    rollout_blocks,
):
    hold_count = lax.axis_size("hold")
    hold_place = lax.axis_index("hold")
    query_tok, grad_tok, out_tok = (
        lax.all_to_all(queries, "bulk", split_axis=1, concat_axis=0, tiled=True),
        lax.all_to_all(out_grad, "bulk", split_axis=1, concat_axis=0, tiled=True),
        lax.all_to_all(attn_out, "bulk", split_axis=1, concat_axis=0, tiled=True),
    )
    kv_dev = prompt_keys.shape[1] // HD
    query_heads = query_tok.reshape(ROWS_DEV, kv_dev, GROUP, HD)
    grad_heads = grad_tok.reshape(ROWS_DEV, kv_dev, GROUP, HD)
    out_heads = out_tok.reshape(ROWS_DEV, kv_dev, GROUP, HD)
    offset_term = jnp.sum(grad_heads.astype(jnp.float32) * out_heads.astype(jnp.float32), axis=-1)
    log_total = log_totals.reshape(ROWS_DEV, kv_dev, GROUP)
    ends = jnp.cumsum(rollout_blocks) * BLOCK
    key_width = PDEV + ROWS_DEV
    key_local = jnp.concatenate([prompt_keys, rollout_keys], 0).reshape(key_width, kv_dev, HD)
    value_local = jnp.concatenate([prompt_values, rollout_values], 0).reshape(key_width, kv_dev, HD)
    own_query_rows = hold_place * ROWS_DEV + jnp.arange(ROWS_DEV, dtype=jnp.int32)
    init = (
        jnp.zeros((ROWS_DEV, kv_dev, GROUP, HD), jnp.float32),
        jnp.zeros((hold_count * key_width, kv_dev, HD), jnp.float32),
        jnp.zeros((hold_count * key_width, kv_dev, HD), jnp.float32),
    )
    key_piece = lax.all_gather(key_local, "hold", axis=0, tiled=True)
    value_piece = lax.all_gather(value_local, "hold", axis=0, tiled=True)
    count = key_piece.shape[0]
    blocks = count // key_width
    columns = jnp.arange(count, dtype=jnp.int32)
    shard_pos = columns // key_width
    within = columns % key_width
    prompt_flag = within < PDEV
    key_rows = shard_pos * ROWS_DEV + within - PDEV

    def one_block(accum, items):
        block_key, block_value, block_flag, block_rows = items
        query_part, key_part, value_part = block_grads(
            query_heads,
            grad_heads,
            log_total,
            offset_term,
            own_query_rows,
            block_key,
            block_value,
            block_flag,
            block_rows,
            ends,
        )
        return (accum + query_part, (key_part, value_part))

    def split(arr):
        return arr.reshape((blocks, key_width) + arr.shape[1:])

    query_acc, (key_part, value_part) = lax.scan(
        one_block,
        init[0],
        (split(key_piece), split(value_piece), split(prompt_flag), split(key_rows)),
    )
    key_part = key_part.reshape((count,) + key_part.shape[2:])
    value_part = value_part.reshape((count,) + value_part.shape[2:])
    key_all = key_part
    value_all = value_part
    query_grad, key_all, value_all = (query_acc, key_all, value_all)
    key_grad, value_grad = (
        lax.psum_scatter(key_all, "hold", scatter_dimension=0, tiled=True),
        lax.psum_scatter(value_all, "hold", scatter_dimension=0, tiled=True),
    )
    query_rounded = query_grad.reshape(ROWS_DEV, kv_dev * GROUP * HD).astype(jnp.bfloat16)
    query_tokens = lax.all_to_all(query_rounded, "bulk", split_axis=0, concat_axis=1, tiled=True)
    key_flat = key_grad.reshape(key_width, kv_dev * HD)
    value_flat = value_grad.reshape(key_width, kv_dev * HD)
    return (query_tokens, key_flat[:PDEV], value_flat[:PDEV], key_flat[PDEV:], value_flat[PDEV:])


def solution(mesh):
    placed = (
        P(("hold", "bulk"), None),
        P(("hold", "bulk"), None),
        P(("hold", "bulk"), None),
        P("hold", "bulk"),
        P("hold", "bulk"),
        P("hold", "bulk"),
        P("hold", "bulk"),
        P("hold", "bulk"),
        P(),
    )
    return jax.shard_map(
        shards,
        mesh=mesh,
        in_specs=placed,
        out_specs=(
            P(("hold", "bulk"), None),
            P("hold", "bulk"),
            P("hold", "bulk"),
            P("hold", "bulk"),
            P("hold", "bulk"),
        ),
        check_vma=False,
    )
```

profile of v0, /device:TPU:0, one launch (start us, length us, event | category | flops | bytes accessed | tf_op | source)
XLA Modules:
  0.0 514.5 jit_solution(1236212018132535579)
XLA Ops:
  12.4 6.3 %all-to-all-start = ((bf16[16,8,1024]{2,0,1:T(8,128)(2,1)}), bf16[16,8,1024]{2,0,1:T(8,128)(2,1)S(1)}, u32[]{:S(2)}, u32[]{:S(2)}) async-start(bf16[16,8,1024]{2,0,1:T(8,128)(2,1)} %bitcast.139), calls=%async_computation | async-start | bytes 524288 | tf_op jit(solution)/shard_map/all_to_all | solution.py:55
  20.4 5.6 %all-to-all-done = bf16[16,8,1024]{2,0,1:T(8,128)(2,1)S(1)} async-done(((bf16[16,8,1024]{2,0,1:T(8,128)(2,1)}), bf16[16,8,1024]{2,0,1:T(8,128)(2,1)S(1)}, u32[]{:S(2)}, u32[]{:S(2)}) %all-to-all-start) | async-done | bytes 262176 | tf_op jit(solution)/shard_map/all_to_all | solution.py:55
  26.0 3.4 all-to-all-start.1
  32.0 4.7 all-to-all-done.1
  36.6 3.4 all-to-all-start.2
  40.4 6.8 %all-to-all-done.2 = bf16[16,8,1024]{2,0,1:T(8,128)(2,1)S(1)} async-done(((bf16[16,8,1024]{2,0,1:T(8,128)(2,1)}), bf16[16,8,1024]{2,0,1:T(8,128)(2,1)S(1)}, u32[]{:S(2)}, u32[]{:S(2)}) %all-to-all-start.2) | async-done | bytes 262176 | tf_op jit(solution)/shard_map/all_to_all | solution.py:57
  47.7 23.1 %all-gather.5.cloned.1.call-done = bf16[18432,128]{1,0:T(8,128)(2,1)} async-done(((bf16[1152,128]{1,0:T(8,128)(2,1)}), bf16[18432,128]{1,0:T(8,128)(2,1)}) %all-gather.5.cloned.1.call-update) | async-done | bytes 4718608 | tf_op jit(solution)/shard_map/all_gather | solution.py:75
  70.8 58.2 %all-gather.7.cloned.1.call-done = bf16[18432,128]{1,0:T(8,128)(2,1)} async-done(((bf16[1152,128]{1,0:T(8,128)(2,1)}), bf16[18432,128]{1,0:T(8,128)(2,1)}) %all-gather.7.cloned.1.call-update) | async-done | bytes 4718608 | tf_op jit(solution)/shard_map/all_gather | solution.py:76
  129.0 160.0 %while.15 = (s32[]{:T(128)}, f32[128,1,8,128]{0,3,2,1:T(8,128)S(1)}, f32[16,1152,1,128]{3,1,2,0:T(8,128)}, f32[16,1152,1,128]{3,1,2,0:T(8,128)}, bf16[16,1152,1,...) while((s32[]{:T(128)}, ...), condition=%wide.region_5.6_spmd.clone, body=%wide.region_2.5_spmd.clone.sunk | while | flops 1519368192 | bytes 25741448 | solution.py:104
  130.3 2.0 bitcast_select_fusion.2
  140.3 2.0 bitcast_select_fusion.2
  150.2 2.0 bitcast_select_fusion.2
  160.3 2.0 bitcast_select_fusion.2
  170.3 2.0 bitcast_select_fusion.2
  180.2 2.0 bitcast_select_fusion.2
  230.2 2.0 bitcast_select_fusion.2
  240.2 2.0 bitcast_select_fusion.2
  250.2 2.0 bitcast_select_fusion.2
  260.2 2.0 bitcast_select_fusion.2
  270.2 2.0 bitcast_select_fusion.2
  280.2 2.0 bitcast_select_fusion.2
  289.9 12.0 %all_to_all.61 = bf16[8,16,1024]{2,1,0:T(8,128)(2,1)S(1)} all-to-all(bf16[8,16,1024]{2,1,0:T(8,128)(2,1)S(1)} %convert_element_type.52), channel_id=1, replica_groups=mesh['hold'=16,'bulk'=8] {'bulk'}, dimensions={0} | all-to-all | bytes 524288 | tf_op jit(solution)/shard_map/all_to_all | solution.py:119
  302.6 91.3 %reduce-scatter.3.cloned.1.call-done = f32[1152,1,128]{2,0,1:T(8,128)} async-done(((f32[18432,1,128]{2,0,1:T(8,128)}), f32[1152,1,128]{2,0,1:T(8,128)}) %reduce-scatter.3.cloned.1.call-update) | async-done | bytes 589840 | tf_op jit(solution)/shard_map/reduce_scatter | solution.py:115
  397.3 107.4 %reduce-scatter.5.cloned.1.call-done = f32[1152,1,128]{2,0,1:T(8,128)} async-done(((f32[18432,1,128]{2,0,1:T(8,128)}), f32[1152,1,128]{2,0,1:T(8,128)}) %reduce-scatter.5.cloned.1.call-update) | async-done | bytes 589840 | tf_op jit(solution)/shard_map/reduce_scatter | solution.py:116
  (218 shorter events, 153.1 us)
Async XLA Ops:
  7.2 63.6 %all-gather.5.cloned.1.call-start = ((), (), s32[]{:S(2)}) async-start(), calls=%async_computation.8 | async-start | bytes 5013504 | tf_op jit(solution)/shard_map/all_gather | solution.py:75
  8.9 120.1 %copy-start = (f32[128,8]{0,1:T(8,128)S(1)}, f32[128,8]{0,1:T(8,128)}, u32[]{:S(2)}) copy-start(f32[128,8]{0,1:T(8,128)} %param.14) | copy-start | bytes 12292
  8.9 120.0 %all-gather.7.cloned.1.call-start = ((), (), s32[]{:S(2)}) async-start(), calls=%async_computation.9 | async-start | bytes 5013504 | tf_op jit(solution)/shard_map/all_gather | solution.py:76
  12.4 13.6 %all-to-all-start = ((bf16[16,8,1024]{2,0,1:T(8,128)(2,1)}), bf16[16,8,1024]{2,0,1:T(8,128)(2,1)S(1)}, u32[]{:S(2)}, u32[]{:S(2)}) async-start(bf16[16,8,1024]{2,0,1:T(8,128)(2,1)} %bitcast.139), calls=%async_computation | async-start | bytes 524288 | tf_op jit(solution)/shard_map/all_to_all | solution.py:55
  26.0 10.6 %all-to-all-start.1 = ((bf16[16,8,1024]{2,0,1:T(8,128)(2,1)}), bf16[16,8,1024]{2,0,1:T(8,128)(2,1)S(1)}, u32[]{:S(2)}, u32[]{:S(2)}) async-start(bf16[16,8,1024]{2,0,1:T(8,128)(2,1)} %bitcast.138), calls=%async_computation.1 | async-start | bytes 524288 | tf_op jit(solution)/shard_map/all_to_all | solution.py:56
  36.6 10.6 %all-to-all-start.2 = ((bf16[16,8,1024]{2,0,1:T(8,128)(2,1)}), bf16[16,8,1024]{2,0,1:T(8,128)(2,1)S(1)}, u32[]{:S(2)}, u32[]{:S(2)}) async-start(bf16[16,8,1024]{2,0,1:T(8,128)(2,1)} %bitcast.137), calls=%async_computation.2 | async-start | bytes 524288 | tf_op jit(solution)/shard_map/all_to_all | solution.py:57
  40.1 353.9 %reduce-scatter.3.cloned.1.call-start = ((), (), s32[]{:S(2)}) async-start(), calls=%async_computation.6 | async-start | bytes 10027008 | tf_op jit(solution)/shard_map/reduce_scatter | solution.py:115
  289.0 215.6 %reduce-scatter.5.cloned.1.call-start = ((), (), s32[]{:S(2)}) async-start(), calls=%async_computation.7 | async-start | bytes 10027008 | tf_op jit(solution)/shard_map/reduce_scatter | solution.py:116
Sparse Core Ops, SparseCore 0:
  11.0 59.6 all-gather.4
  73.8 55.1 all-gather.6
  289.1 104.7 reduce-scatter.2
  398.7 105.8 reduce-scatter.4
where the time goes:
time: 517 us; the launch traced here: 515 us
  waiting for transfers between devices  298 us (58%)
  matrix products  138 us (27%)
  other arithmetic  25 us (5%)
  local copies, waits for them, and re-layouts  13.9 us (3%)
  between operations  13.9 us (3%)
  starting transfers between devices  13.3 us (3%)
  blocking collectives  12 us (2%)
    reduce_scatter x1, waiting for transfers between devices, shards(): lax.psum_scatter(value_all, 'hold', scatter_dimension=0, tiled=True)  107 us
    reduce_scatter x1, waiting for transfers between devices, shards(): lax.psum_scatter(key_all, 'hold', scatter_dimension=0, tiled=True)  91.3 us
    all_gather x1, waiting for transfers between devices, shards(): value_piece = lax.all_gather(value_local, 'hold', axis=0, tiled=True)  58.2 us
    dot_general x16, matrix products, block_grads(): jnp.einsum('nkgd,mkd->nkgm', query, keys, preferred_element_type=jnp.floa...  32.8 us
    dot_general x16, matrix products, block_grads(): jnp.einsum('nkgd,mkd->nkgm', grad_out, values, preferred_element_type=jnp...  28.1 us
    dot_general x16, matrix products, block_grads(): jnp.einsum('nkgm,nkgd->mkd', prob_b, grad_out, preferred_element_type=jnp...  25.9 us
    dot_general x16, matrix products, block_grads(): jnp.einsum('nkgm,nkgd->mkd', dscore, query, preferred_element_type=jnp.fl...  25.8 us
    dot_general x16, matrix products, block_grads(): jnp.einsum('nkgm,mkd->nkgd', dscore, keys, preferred_element_type=jnp.flo...  25.4 us
  transfers between devices with their start and end apart: 7, of which 7 were waited for; matrix products, arithmetic and copies ran while one was open for 2% of the time, Pallas kernels for 0%

commit v1 on v0

v1 whole, which is shorter than its diff:
```python
import functools

import jax
import jax.numpy as jnp
from jax import lax
from jax.experimental import pallas as pl
from jax.experimental.pallas import tpu as pltpu
from jax.sharding import Mesh
from jax.sharding import PartitionSpec as P

F32 = jnp.float32
BF16 = jnp.bfloat16
HD = 128
GROUP = 8
BLOCK = 128
NBLK = 16
PK = 1024
RK = 128
KW = PK + RK
QR = BLOCK * GROUP
SRC = 8
SUB = BLOCK // SRC
PAY = 2 * BLOCK + 16
SCALE = HD ** (-0.5)
LOG2E = 1.4426950408889634
C2 = SCALE * LOG2E

NN = (((1,), (0,)), ((), ()))
NT = (((1,), (1,)), ((), ()))

Y, XH, C, Z, XL = "y", "xh", "c", "z", "xl"
BULK = (Z, XL)


def dot(a, b, dims):
    return lax.dot_general(a, b, dims, preferred_element_type=F32)


def pack_kernel(q, g, o, pk, rk, pv, rv, pay, kv, sems):
    copies, at = [], 0
    for n, (src, rows) in enumerate(((pk, PK), (rk, RK), (pv, PK), (rv, RK))):
        copies.append(pltpu.make_async_copy(src, kv.at[pl.ds(at, rows)], sems.at[n]))
        at += rows
    for copy in copies:
        copy.start()
    ones = jnp.ones((16, HD), BF16)
    row = lax.broadcasted_iota(jnp.int32, (16, BLOCK), 0)
    for b in range(SRC):
        prods = []
        for h in range(GROUP):
            cols = slice((b * GROUP + h) * HD, (b * GROUP + h + 1) * HD)
            qh, gh = q[:, cols], g[:, cols]
            pay[b, h * SUB : (h + 1) * SUB, :] = qh
            pay[b, BLOCK + h * SUB : BLOCK + (h + 1) * SUB, :] = gh
            prods.append(gh.astype(F32) * o[:, cols].astype(F32))
        prod = jnp.concatenate(prods, axis=0)
        high = prod.astype(BF16)
        low = (prod - high.astype(F32)).astype(BF16)
        delta = dot(ones, high, NT) + dot(ones, low, NT)
        d1 = delta.astype(BF16).astype(F32)
        d2 = (delta - d1).astype(BF16).astype(F32)
        d3 = delta - d1 - d2
        pieces = jnp.where(row == 0, d1, jnp.where(row == 1, d2, jnp.where(row == 2, d3, 0.0)))
        pay[b, 2 * BLOCK : PAY, :] = pieces.astype(BF16)
    for copy in copies:
        copy.wait()


def pack(q, g, o, pk, rk, pv, rv):
    anyspec = pl.BlockSpec(memory_space=pl.ANY)
    vspec = pl.BlockSpec(memory_space=pltpu.VMEM)
    return pl.pallas_call(
        pack_kernel,
        in_specs=[vspec] * 3 + [anyspec] * 4,
        out_specs=[vspec, anyspec],
        out_shape=[
            jax.ShapeDtypeStruct((SRC, PAY, HD), BF16),
            jax.ShapeDtypeStruct((2 * KW, HD), BF16),
        ],
        scratch_shapes=[pltpu.SemaphoreType.DMA((4,))],
        compiler_params=pltpu.CompilerParams(vmem_limit_bytes=16 << 20),
        name="pack",
    )(q, g, o, pk, rk, pv, rv)


def row_vector(rows):
    return jnp.concatenate([rows[s : s + 1, :] for s in range(SRC)], axis=1)


def column(rows):
    return jnp.broadcast_to(row_vector(rows), (HD, QR)).T


def tiles_kernel(cfg, *refs):
    unit, keys_of, kv_in, dq_in, final = cfg
    nk = len(keys_of)
    refs = list(refs)

    def take(n):
        out = refs[:n]
        del refs[:n]
        return out

    place, lengths, logs = take(3)
    pay_in = take(1 if unit == "own" else 2)
    dq_src = take(1) if dq_in else []
    key_in = take(nk)
    kv_src = dict(zip([n for n in range(nk) if kv_in[n]], take(sum(kv_in))))
    halves = final and unit in ("near_a", "near_b")
    dq_out = take(2 if halves else 1)
    kv_out = take(nk)
    pay, keys, acc, dqa, sem_q, sem_k, sem_a, sem_o = refs

    loads = []
    if unit == "own":
        loads.append(pltpu.make_async_copy(pay_in[0], pay, sem_q.at[0]))
    else:
        for h in range(2):
            loads.append(pltpu.make_async_copy(pay_in[h], pay.at[pl.ds(4 * h, 4)], sem_q.at[h]))
    if dq_in:
        loads.append(pltpu.make_async_copy(dq_src[0], dqa, sem_q.at[2]))
    for copy in loads:
        copy.start()
    for n in range(nk):
        pltpu.make_async_copy(key_in[n], keys.at[n], sem_k.at[n]).start()
        if kv_in[n]:
            pltpu.make_async_copy(kv_src[n], acc.at[n], sem_a.at[n]).start()
        else:
            acc[n] = jnp.zeros((2 * HD, KW), F32)
    if not dq_in:
        dqa[...] = jnp.zeros((QR, HD), F32)

    y, xh, c = place[0], place[1], place[2]
    if unit == "own":
        log_rows = logs[0] if logs.shape[0] == 1 else logs[y]
    elif unit == "opp":
        log_rows = logs[(y + 2) % 4]
    else:
        up, down = logs[(y + 1) % 4], logs[(y + 3) % 4]
        parts = [up[0:4], down[4:8]] if unit == "near_a" else [up[4:8], down[0:4]]
        log_rows = jnp.concatenate(parts, axis=0)
    log_col = column(log_rows)
    for copy in loads:
        copy.wait()
    pieces = pay[:, 2 * BLOCK : PAY, :].astype(F32)
    delta_col = column(pieces[:, 0, :] + pieces[:, 1, :] + pieces[:, 2, :])
    q = pay[:, 0:BLOCK, :].reshape(QR, HD)
    g = pay[:, BLOCK : 2 * BLOCK, :].reshape(QR, HD)
    qt, gt = q.T, g.T

    def step(j, carry):
        pltpu.make_async_copy(key_in[0], keys.at[j], sem_k.at[j]).wait()
        for n in range(nk):
            if kv_in[n]:

                @pl.when(j == n)
                def _():
                    pltpu.make_async_copy(kv_src[n], acc.at[n], sem_a.at[n]).wait()

        def products(at, width, rows):
            s = dot(q[:rows], keys[j, at : at + width, :], NT)
            dp = dot(g[:rows], keys[j, KW + at : KW + at + width, :], NT)
            return s, dp

        def grads(at, width, rows, s, dp, allowed):
            wide = lambda col: jnp.concatenate([col[:rows]] * (width // HD), axis=1)
            p = jnp.exp2(s * C2 - wide(log_col))
            if allowed is not None:
                p = jnp.where(allowed, p, 0.0)
            ds = (p * (dp - wide(delta_col))).astype(BF16)
            p = p.astype(BF16)
            acc[j, 0:HD, at : at + width] += dot(qt[:, :rows], ds, NN)
            acc[j, HD : 2 * HD, at : at + width] += dot(gt[:, :rows], p, NN)
            return dot(ds, keys[j, at : at + width, :], NN)

        part = 256
        total = None
        ahead = products(0, part, QR)
        for n in range(PK // part):
            s, dp = ahead
            if n + 1 < PK // part:
                ahead = products((n + 1) * part, part, QR)
            term = grads(n * part, part, QR, s, dp, None)
            total = term if total is None else total + term
        dqa[...] += total

        if unit != "opp":
            rows = QR if unit == "own" else QR // 2
            qi = 4 * (y if unit == "own" else (y + 1) % 4) + 2 * xh + c
            fx = sum(jnp.where(j == n, keys_of[n][0], 0) for n in range(nk))
            fc = sum(jnp.where(j == n, keys_of[n][1], 0) for n in range(nk))
            kj = 4 * y + 2 * (xh + fx - 2 * xh * fx) + (c + fc - 2 * c * fc)
            seen, end = kj <= qi, 0
            for r in range(lengths.shape[0]):
                end = end + lengths[r]
                seen = seen & ((end <= kj) | (end > qi))

            @pl.when(seen)
            def _():
                allowed = None
                if unit == "own":
                    row = lax.broadcasted_iota(jnp.int32, (rows, RK), 0)
                    key_at = lax.broadcasted_iota(jnp.int32, (rows, RK), 1)
                    token = (row // BLOCK) * SUB + row % SUB
                    allowed = (kj < qi) | (key_at <= token)
                s, dp = products(PK, RK, rows)
                dqa[:rows, :] += grads(PK, RK, rows, s, dp, allowed)

        for n in range(nk):

            @pl.when(j == n)
            def _():
                pltpu.make_async_copy(acc.at[n], kv_out[n], sem_o.at[n]).start()

        return carry

    lax.fori_loop(0, nk, step, 0)
    if final and unit != "own":
        done = (dqa[...] * SCALE).astype(BF16).reshape(SRC, BLOCK, HD)
        if halves:
            dq_out[0][...], dq_out[1][...] = done[0:4], done[4:8]
        else:
            dq_out[0][...] = done
    else:
        dq_out[0][...] = dqa[...]
    for n in range(nk):
        pltpu.make_async_copy(acc.at[n], kv_out[n], sem_o.at[n]).wait()


def tiles(name, unit, common, pays, keys_of, keys, sums, dq=None, final=False):
    nk = len(keys)
    kv_in = tuple(g is not None for g in sums)
    cfg = (unit, tuple(keys_of), kv_in, dq is not None, final)
    anyspec = pl.BlockSpec(memory_space=pl.ANY)
    vspec = pl.BlockSpec(memory_space=pltpu.VMEM)
    sspec = pl.BlockSpec(memory_space=pltpu.SMEM)
    operands = list(common) + list(pays) + ([dq] if dq is not None else []) + list(keys)
    specs = [sspec, sspec, vspec] + [anyspec] * (len(operands) - 3)
    if not final or unit == "own":
        dq_shapes = [jax.ShapeDtypeStruct((QR, HD), F32)]
    elif unit == "opp":
        dq_shapes = [jax.ShapeDtypeStruct((SRC, BLOCK, HD), BF16)]
    else:
        dq_shapes = [jax.ShapeDtypeStruct((SRC // 2, BLOCK, HD), BF16)] * 2
    aliases = {}
    for n in range(nk):
        if kv_in[n]:
            aliases[len(operands)] = len(dq_shapes) + n
            operands.append(sums[n])
            specs.append(anyspec)
    outs = pl.pallas_call(
        functools.partial(tiles_kernel, cfg),
        in_specs=specs,
        out_specs=[vspec] * len(dq_shapes) + [anyspec] * nk,
        out_shape=dq_shapes + [jax.ShapeDtypeStruct((2 * HD, KW), F32)] * nk,
        scratch_shapes=[
            pltpu.VMEM((SRC, PAY, HD), BF16),
            pltpu.VMEM((nk, 2 * KW, HD), BF16),
            pltpu.VMEM((nk, 2 * HD, KW), F32),
            pltpu.VMEM((QR, HD), F32),
            pltpu.SemaphoreType.DMA((3,)),
            pltpu.SemaphoreType.DMA((nk,)),
            pltpu.SemaphoreType.DMA((nk,)),
            pltpu.SemaphoreType.DMA((nk,)),
        ],
        input_output_aliases=aliases,
        compiler_params=pltpu.CompilerParams(vmem_limit_bytes=40 << 20),
        cost_estimate=pl.CostEstimate(
            flops=nk * 10 * QR * PK * HD, bytes_accessed=4 << 20, transcendentals=0
        ),
        name=name,
    )(*operands)
    dqs, sums = outs[: len(dq_shapes)], outs[len(dq_shapes) :]
    return (dqs[0] if len(dqs) == 1 else dqs), sums


def finish_kernel(own, up_a, up_b, down_a, down_b, opp, out):
    for s in range(SRC):
        up, down = (up_a, down_a) if s < 4 else (up_b, down_b)
        rows = own[s * BLOCK : (s + 1) * BLOCK, :] * SCALE
        rows = rows + up[s % 4].astype(F32) + down[s % 4].astype(F32) + opp[s].astype(F32)
        out[s] = rows.astype(BF16)


def finish(*terms):
    return pl.pallas_call(
        finish_kernel, out_shape=jax.ShapeDtypeStruct((SRC, BLOCK, HD), BF16), name="finish"
    )(*terms)


def close_kernel(own, core, chip, dk, dv, drk, drv):
    def total(rows, cols):
        part = own[rows, cols] + core[rows, cols] + chip[rows, cols].astype(F32)
        return part.T

    keys, values = slice(0, HD), slice(HD, 2 * HD)
    dk[...] = total(keys, slice(0, PK)) * SCALE
    drk[...] = total(keys, slice(PK, KW)) * SCALE
    dv[...] = total(values, slice(0, PK))
    drv[...] = total(values, slice(PK, KW))


def close(own, core, chip):
    shape = lambda rows: jax.ShapeDtypeStruct((rows, HD), F32)
    return pl.pallas_call(
        close_kernel, out_shape=[shape(PK), shape(PK), shape(RK), shape(RK)], name="close"
    )(own, core, chip)


def shift(n, s):
    return [(i, (i + s) % n) for i in range(n)]


def after(values, *earlier):
    return lax.optimization_barrier((values, earlier))[0]


def shards(
    queries,
    out_grad,
    attn_out,
    log_totals,
    prompt_keys,
    prompt_values,
    rollout_keys,
    rollout_values,
    rollout_blocks,
):
    place = jnp.stack([lax.axis_index(Y), lax.axis_index(XH), lax.axis_index(C)])
    place = place.astype(jnp.int32)
    to_next, to_last = shift(4, 1), shift(4, -1)
    swap = shift(2, 1)

    l0 = (log_totals * LOG2E).reshape(SRC, SUB, GROUP).transpose(0, 2, 1).reshape(SRC, BLOCK)
    l_all = lax.all_gather(l0, Y, axis=0, tiled=False)

    payload, kv_own = pack(
        queries, out_grad, attn_out, prompt_keys, rollout_keys, prompt_values, rollout_values
    )
    kv_x = lax.ppermute(kv_own, XH, swap)
    kv_c = lax.ppermute(kv_own, C, swap)
    kv_xc = lax.ppermute(kv_x, C, swap)
    own = lax.all_to_all(payload, BULK, split_axis=0, concat_axis=0, tiled=True)
    own_a, own_b = own[:4], own[4:]
    up_a = lax.ppermute(own_a, Y, to_last)
    down_b = lax.ppermute(own_b, Y, to_next)
    up_b = lax.ppermute(own_b, Y, to_last)
    down_a = lax.ppermute(own_a, Y, to_next)

    far, near = [(1, 0), (1, 1)], [(0, 0), (0, 1)]
    first, common = (place, rollout_blocks, l0[None]), (place, rollout_blocks, l_all)

    dq_own, (g_x, g_xc, g_c) = tiles(
        "own_3", "own", first, [own], far + near[1:], [kv_x, kv_xc, kv_c], [None] * 3
    )
    up_a, down_b = after((up_a, down_b), dq_own)
    opp_a = lax.ppermute(up_a, Y, to_last)
    opp_b = lax.ppermute(down_b, Y, to_next)
    dq_a, (g_x, g_xc) = tiles(
        "a_far", "near_a", common, [up_a, down_b], far, [kv_x, kv_xc], [g_x, g_xc]
    )
    up_b, down_a = after((up_b, down_a), dq_a)
    dq_b, (g_x, g_xc) = tiles(
        "b_far", "near_b", common, [up_b, down_a], far, [kv_x, kv_xc], [g_x, g_xc]
    )
    dq_a = after(dq_a, dq_b)
    (a_up, a_down), (g_own, g_c) = tiles(
        "a_near", "near_a", common, [up_a, down_b], near, [kv_own, kv_c], [None, g_c], dq_a, True
    )
    from_a_down = lax.ppermute(a_up, Y, to_next)
    from_a_up = lax.ppermute(a_down, Y, to_last)
    opp_a, opp_b = after((opp_a, opp_b), a_up)
    dq_opp, (g_x, g_xc) = tiles(
        "opp_far", "opp", common, [opp_a, opp_b], far, [kv_x, kv_xc], [g_x, g_xc]
    )
    from_core = lax.ppermute(g_xc, C, swap)
    opp, (g_own, g_c) = tiles(
        "opp_near", "opp", common, [opp_a, opp_b], near, [kv_own, kv_c], [g_own, g_c], dq_opp, True
    )
    from_opp = lax.ppermute(opp, Y, shift(4, 2))
    to_chip = (g_x + after(from_core, opp)).astype(BF16)
    from_chip = lax.ppermute(to_chip, XH, swap)
    dq_b = after(dq_b, to_chip)
    (b_up, b_down), (g_own, g_c) = tiles(
        "b_near", "near_b", common, [up_b, down_a], near, [kv_own, kv_c], [g_own, g_c], dq_b, True
    )
    from_b_down = lax.ppermute(b_up, Y, to_next)
    from_b_up = lax.ppermute(b_down, Y, to_last)
    from_c = lax.ppermute(g_c, C, swap)
    dq_own, (g_own,) = tiles(
        "own_1", "own", common, [own], near[:1], [kv_own], [g_own], dq_own, True
    )

    dq = finish(dq_own, from_b_up, from_a_up, from_a_down, from_b_down, from_opp)
    dq = lax.all_to_all(dq, BULK, split_axis=0, concat_axis=0, tiled=True)
    query_grad = dq.reshape(SRC * GROUP, SUB, HD).transpose(1, 0, 2).reshape(SUB, SRC * GROUP * HD)
    dk, dv, drk, drv = close(g_own, from_c, from_chip)
    return (query_grad, dk, dv, drk, drv)


def solution(mesh):
    fine = Mesh(mesh.devices.reshape(4, 2, 2, 4, 2), (Y, XH, C, Z, XL))
    hold, bulk = (Y, XH, C), (Z, XL)
    tokens = P(hold + bulk, None)
    split = P(hold, bulk)
    return jax.shard_map(
        shards,
        mesh=fine,
        in_specs=(tokens, tokens, tokens, split, split, split, split, split, P()),
        out_specs=(tokens, split, split, split, split),
        check_vma=False,
    )
```

time: 517 us -> 152 us (0.29)
  waiting for transfers between devices: 298 us -> 16.6 us
  matrix products: 138 us -> 0 us
  Pallas kernels: 0 us -> 67.3 us
  other arithmetic: 25 us -> 1 us
  starting transfers between devices: 13.3 us -> 26.9 us
  blocking collectives: 12 us -> 25.1 us
  between operations: 13.9 us -> 0.92 us
    reduce_scatter x2 -> x0, waiting for transfers between devices: 199 us -> none  [the longest x1 107 us: shards(): lax.psum_scatter(value_all, 'hold', scatter_dimension=0, tiled=True)]
    dot_general x80 -> x0, matrix products: 138 us -> none  [the longest x16 32.8 us: block_grads(): jnp.einsum('nkgd,mkd->nkgm', query, keys, preferred_element_type=jnp.floa...]
    all_gather x2 -> x0, waiting for transfers between devices: 81.3 us -> none  [the longest x1 58.2 us: shards(): value_piece = lax.all_gather(value_local, 'hold', axis=0, tiled=True)]
    pallas_call x0 -> x11, Pallas kernels: none -> 67.3 us  [the longest x8 60.8 us: tiles(): pl.pallas_call(functools.partial(tiles_kernel, cfg), in_specs=specs, out_...]
    ppermute x0 -> x17, starting transfers between devices: none -> 21.4 us  [the longest x1 3.54 us: shards(): from_chip = lax.ppermute(to_chip, XH, swap)]
    or x16 -> x0, other arithmetic: 17.4 us -> none  [block_grads(): key_prompt[None, :]]
    all_to_all x3 -> x1, waiting for transfers between devices: 17.1 us -> 0.01 us  [shards(): own = lax.all_to_all(payload, BULK, split_axis=0, concat_axis=0, tiled=True)]
    ppermute x0 -> x17, waiting for transfers between devices: none -> 16.6 us  [the longest x1 9.15 us: shards(): kv_x = lax.ppermute(kv_own, XH, swap)]
  transfers between devices with their start and end apart: 7 -> 18, of which waited for: 7 -> 3; matrix products, arithmetic and copies ran while one was open for 2% -> 1% of each run, Pallas kernels for 0% -> 32%
where the time goes in v1:
time: 152 us; the launch traced here: 151 us
  Pallas kernels  67.3 us (44%)
  starting transfers between devices  26.9 us (18%)
  blocking collectives  25.1 us (17%)
  waiting for transfers between devices  16.6 us (11%)
  local copies, waits for them, and re-layouts  13 us (9%)
    pallas_call x8, Pallas kernels, tiles(): pl.pallas_call(functools.partial(tiles_kernel, cfg), in_specs=specs, out_...  60.8 us
    all_to_all x1, blocking collectives, shards(): dq = lax.all_to_all(dq, BULK, split_axis=0, concat_axis=0, tiled=True)  12.6 us
    all_gather x1, blocking collectives, shards(): l_all = lax.all_gather(l0, Y, axis=0, tiled=False)  12.5 us
    unnamed x48, local copies, waits for them, and re-layouts  12.1 us
    ppermute x1, waiting for transfers between devices, shards(): kv_x = lax.ppermute(kv_own, XH, swap)  9.15 us
    all_to_all x1, starting transfers between devices, shards(): own = lax.all_to_all(payload, BULK, split_axis=0, concat_axis=0, tiled=True)  5.47 us
    ppermute x1, waiting for transfers between devices, shards(): from_a_down = lax.ppermute(a_up, Y, to_next)  5.34 us
    ppermute x1, starting transfers between devices, shards(): from_chip = lax.ppermute(to_chip, XH, swap)  3.54 us
  transfers between devices with their start and end apart: 18, of which 3 were waited for; matrix products, arithmetic and copies ran while one was open for 1% of the time, Pallas kernels for 32%

profile of v1, /device:TPU:0, one launch (start us, length us, event | category | flops | bytes accessed | tf_op | source)
XLA Modules:
  0.0 150.9 jit_solution(6860866279373133563)
XLA Ops:
  6.9 1.4 pack.1
  8.3 3.2 %collective-permute-start = (bf16[2304,128]{1,0:T(8,128)(2,1)S(1)}, bf16[2304,128]{1,0:T(8,128)(2,1)S(1)}, u32[]{:S(2)}, u32[]{:S(2)}) collective-permute-start(bf16[2304,128]{1,0:T(8,128)(2,1)S(1)} %get-tuple-element.47.refs_6_.refs_5_), channel_id=1, source_target_pairs={{0,16},{16,0},{1,17},{17,1},{2,18},{18,2},{3,19},{19,3},{4,20},{20... | collective-permute-start | bytes 1769480 | tf_op jit(solution)/shard_map/ppermute | solution.py:340
  11.5 5.5 %all-to-all-start = ((bf16[8,272,128]{2,1,0:T(8,128)(2,1)}), bf16[8,272,128]{2,1,0:T(8,128)(2,1)S(1)}, u32[]{:S(2)}, u32[]{:S(2)}) async-start(bf16[8,272,128]{2,1,0:T(8,128)(2,1)} %get-tuple-element.46), calls=%async_computation | async-start | bytes 1114112 | tf_op jit(solution)/shard_map/all_to_all | solution.py:343
  17.0 9.1 %collective-permute-done.refs_4_.refs_5_ = bf16[2304,128]{1,0:T(8,128)(2,1)S(1)} collective-permute-done((bf16[2304,128]{1,0:T(8,128)(2,1)S(1)}, bf16[2304,128]{1,0:T(8,128)(2,1)S(1)}, u32[]{:S(2)}, u32[]{:S(2)}) %collective-permute-start) | collective-permute-done | bytes 589856 | tf_op jit(solution)/shard_map/ppermute | solution.py:340
  26.3 12.5 %all_gather.3.refs_2_ = f32[4,8,128]{2,1,0:T(8,128)S(1)} all-gather(f32[1,8,128]{2,1,0:T(8,128)S(1)} %all_gather_reshape.3.refs_2_), channel_id=1, replica_groups=mesh['y'=4,'xh'=2,'c'=2,'z'=4,'xl'=2] {'y'}, dimensions={0}, use_global_device_ids=true | all-gather | bytes 20480 | tf_op jit(solution)/shard_map/all_gather | solution.py:335
  38.9 2.6 %collective-permute-start.5 = (bf16[4,272,128]{2,1,0:T(8,128)(2,1)S(1)}, bf16[4,272,128]{2,1,0:T(8,128)(2,1)S(1)}, u32[]{:S(2)}, u32[]{:S(2)}) collective-permute-start(bf16[4,272,128]{2,1,0:T(8,128)(2,1)S(1)} %get-tuple-element.87), channel_id=1, source_target_pairs={{0,96},{32,0},{64,32},{96,64},{1,97},{33,1},{65,33},{97,65},{2,98}... | collective-permute-start | bytes 835592 | tf_op jit(solution)/shard_map/ppermute | solution.py:345
  42.3 2.5 %collective-permute-start.3 = (bf16[4,272,128]{2,1,0:T(8,128)(2,1)S(1)}, bf16[4,272,128]{2,1,0:T(8,128)(2,1)S(1)}, u32[]{:S(2)}, u32[]{:S(2)}) collective-permute-start(bf16[4,272,128]{2,1,0:T(8,128)(2,1)S(1)} %get-tuple-element.88), channel_id=1, source_target_pairs={{0,96},{32,0},{64,32},{96,64},{1,97},{33,1},{65,33},{97,65},{2,98}... | collective-permute-start | bytes 835592 | tf_op jit(solution)/shard_map/ppermute | solution.py:347
  47.8 9.9 %own_3.1 = (f32[1024,128]{1,0:T(8,128)S(1)}, f32[256,1152]{1,0:T(8,128)S(1)}, f32[256,1152]{1,0:T(8,128)S(1)}, f32[256,1152]{1,0:T(8,128)S(1)}) custom-call(s32[3]{0:T(128)S(1)} %pad_add_fusion.refs_0_, s32[8]{0:T(128)S(1)} %copy-done.17, f32[1,8,128]{2,1,0:T(8,128)S(1)} %all_gather_reshape.3.refs_2_, bf16[8,272,128]{2,1,0:T(8,128)(2,1)S(1)} %all-to-all-done.refs_3_, ...), custom_call_target="tpu_custom_call" | custom-call | flops 4026531840 | bytes 4194304 | tf_op jit(solution)/shard_map/own_3/pallas_call | solution.py:251
  57.8 2.0 %collective-permute-start.7 = (bf16[4,272,128]{2,1,0:T(8,128)(2,1)S(1)}, bf16[4,272,128]{2,1,0:T(8,128)(2,1)S(1)}, u32[]{:S(2)}, u32[]{:S(2)}) collective-permute-start(bf16[4,272,128]{2,1,0:T(8,128)(2,1)S(1)} %collective-permute-done.5.refs_3_), channel_id=1, source_target_pairs={{0,96},{32,0},{64,32},{96,64},{1,97},{33,1},{65,33},{97,65},{2,98}... | collective-permute-start | bytes 835592 | tf_op jit(solution)/shard_map/ppermute | solution.py:357
  59.9 7.9 %a_far.1 = (f32[1024,128]{1,0:T(8,128)S(1)}, f32[256,1152]{1,0:T(8,128)S(1)}, f32[256,1152]{1,0:T(8,128)S(1)}) custom-call(s32[3]{0:T(128)S(1)} %pad_add_fusion.refs_0_, s32[8]{0:T(128)S(1)} %copy-done.17, f32[4,8,128]{2,1,0:T(8,128)S(1)} %all_gather.3.refs_2_, ...), custom_call_target="tpu_custom_call", output_to_operand_aliasing={{1}: (7, {}), {2}: (8, {})} | custom-call | flops 2684354560 | bytes 4194304 | tf_op jit(solution)/shard_map/a_far/pallas_call | solution.py:251
  67.8 7.9 %b_far.1 = (f32[1024,128]{1,0:T(8,128)S(1)}, f32[256,1152]{1,0:T(8,128)S(1)}, f32[256,1152]{1,0:T(8,128)S(1)}) custom-call(s32[3]{0:T(128)S(1)} %pad_add_fusion.refs_0_, s32[8]{0:T(128)S(1)} %copy-done.17, f32[4,8,128]{2,1,0:T(8,128)S(1)} %all_gather.3.refs_2_, ...), custom_call_target="tpu_custom_call", output_to_operand_aliasing={{1}: (7, {}), {2}: (8, {})} | custom-call | flops 2684354560 | bytes 4194304 | tf_op jit(solution)/shard_map/b_far/pallas_call | solution.py:251
  75.8 7.3 %a_near.1 = (bf16[4,128,128]{2,1,0:T(8,128)(2,1)S(1)}, bf16[4,128,128]{2,1,0:T(8,128)(2,1)S(1)}, f32[256,1152]{1,0:T(8,128)S(1)}, f32[256,1152]{1,0:T(8,128)S(1)}) custom-call(s32[3]{0:T(128)S(1)} %pad_add_fusion.refs_0_, s32[8]{0:T(128)S(1)} %copy-done.17, f32[4,8,128]{2,1,0:T(8,128)S(1)} %all_gather.3.refs_2_, ...), custom_call_target="tpu_custom_call", output_to_operand_aliasing={{3}: (8, {})} | custom-call | flops 2684354560 | bytes 4194304 | tf_op jit(solution)/shard_map/a_near/pallas_call | solution.py:251
  83.1 7.6 %opp_far.1 = (f32[1024,128]{1,0:T(8,128)S(1)}, f32[256,1152]{1,0:T(8,128)S(1)}, f32[256,1152]{1,0:T(8,128)S(1)}) custom-call(s32[3]{0:T(128)S(1)} %pad_add_fusion.refs_0_, s32[8]{0:T(128)S(1)} %copy-done.17, f32[4,8,128]{2,1,0:T(8,128)S(1)} %all_gather.3.refs_2_, ...), custom_call_target="tpu_custom_call", output_to_operand_aliasing={{1}: (7, {}), {2}: (8, {})} | custom-call | flops 2684354560 | bytes 4194304 | tf_op jit(solution)/shard_map/opp_far/pallas_call | solution.py:251
  90.8 7.4 %opp_near.1 = (bf16[8,128,128]{2,1,0:T(8,128)(2,1)S(1)}, f32[256,1152]{1,0:T(8,128)S(1)}, f32[256,1152]{1,0:T(8,128)S(1)}) custom-call(s32[3]{0:T(128)S(1)} %pad_add_fusion.refs_0_, s32[8]{0:T(128)S(1)} %copy-done.17, f32[4,8,128]{2,1,0:T(8,128)S(1)} %all_gather.3.refs_2_, ...), custom_call_target="tpu_custom_call", output_to_operand_aliasing={{1}: (8, {}), {2}: (9, {})} | custom-call | flops 2684354560 | bytes 4194304 | tf_op jit(solution)/shard_map/opp_near/pallas_call | solution.py:251
  99.2 7.5 %b_near.1 = (bf16[4,128,128]{2,1,0:T(8,128)(2,1)S(1)}, bf16[4,128,128]{2,1,0:T(8,128)(2,1)S(1)}, f32[256,1152]{1,0:T(8,128)S(1)}, f32[256,1152]{1,0:T(8,128)S(1)}) custom-call(s32[3]{0:T(128)S(1)} %pad_add_fusion.refs_0_, s32[8]{0:T(128)S(1)} %copy-done.17, f32[4,8,128]{2,1,0:T(8,128)S(1)} %all_gather.3.refs_2_, ...), custom_call_target="tpu_custom_call", output_to_operand_aliasing={{2}: (8, {}), {3}: (9, {})} | custom-call | flops 2684354560 | bytes 4194304 | tf_op jit(solution)/shard_map/b_near/pallas_call | solution.py:251
  107.2 3.5 %collective-permute-start.16 = (bf16[256,1152]{1,0:T(8,128)(2,1)}, bf16[256,1152]{1,0:T(8,128)(2,1)}, u32[]{:S(2)}, u32[]{:S(2)}) collective-permute-start(bf16[256,1152]{1,0:T(8,128)(2,1)} %add_convert_fusion), channel_id=1, source_target_pairs={{0,16},{16,0},{1,17},{17,1},{2,18},{18,2},{3,19},{19,3},{4,20},{20... | collective-permute-start | bytes 1769480 | tf_op jit(solution)/shard_map/ppermute | solution.py:382
  110.8 1.7 %collective-permute-start.11 = (bf16[4,128,128]{2,1,0:T(8,128)(2,1)S(1)}, bf16[4,128,128]{2,1,0:T(8,128)(2,1)S(1)}, u32[]{:S(2)}, u32[]{:S(2)}) collective-permute-start(bf16[4,128,128]{2,1,0:T(8,128)(2,1)S(1)} %get-tuple-element.79), channel_id=1, source_target_pairs={{0,96},{32,0},{64,32},{96,64},{1,97},{33,1},{65,33},{97,65},{2,98}... | collective-permute-start | bytes 393224 | tf_op jit(solution)/shard_map/ppermute | solution.py:371
  113.9 2.1 %collective-permute-done.11.up_b = bf16[4,128,128]{2,1,0:T(8,128)(2,1)S(1)} collective-permute-done((bf16[4,128,128]{2,1,0:T(8,128)(2,1)S(1)}, bf16[4,128,128]{2,1,0:T(8,128)(2,1)S(1)}, u32[]{:S(2)}, u32[]{:S(2)}) %collective-permute-start.11) | collective-permute-done | bytes 131104 | tf_op jit(solution)/shard_map/ppermute | solution.py:371
  116.0 2.9 %collective-permute-start.10 = (bf16[4,128,128]{2,1,0:T(8,128)(2,1)S(1)}, bf16[4,128,128]{2,1,0:T(8,128)(2,1)S(1)}, u32[]{:S(2)}, u32[]{:S(2)}) collective-permute-start(bf16[4,128,128]{2,1,0:T(8,128)(2,1)S(1)} %get-tuple-element.78), channel_id=1, source_target_pairs={{0,96},{32,0},{64,32},{96,64},{1,97},{33,1},{65,33},{97,65},{2,98}... | collective-permute-start | bytes 393224 | tf_op jit(solution)/shard_map/ppermute | solution.py:388
  118.9 5.3 %collective-permute-done.12.down_a = bf16[4,128,128]{2,1,0:T(8,128)(2,1)S(1)} collective-permute-done((bf16[4,128,128]{2,1,0:T(8,128)(2,1)S(1)}, bf16[4,128,128]{2,1,0:T(8,128)(2,1)S(1)}, u32[]{:S(2)}, u32[]{:S(2)}) %collective-permute-start.12) | collective-permute-done | bytes 131104 | tf_op jit(solution)/shard_map/ppermute | solution.py:370
  124.9 5.3 %own_1.1 = (f32[1024,128]{1,0:T(8,128)S(1)}, f32[256,1152]{1,0:T(8,128)S(1)}) custom-call(s32[3]{0:T(128)S(1)} %pad_add_fusion.refs_0_, s32[8]{0:T(128)S(1)} %copy-done.17, f32[4,8,128]{2,1,0:T(8,128)S(1)} %all_gather.3.refs_2_, bf16[8,272,128]{2,1,0:T(8,128)(2,1)S(1)} %all-to-all-done.refs_3_, ...), custom_call_target="tpu_custom_call", output_to_operand_aliasing={{1}: (6, {})} | custom-call | flops 1342177280 | bytes 4194304 | tf_op jit(solution)/shard_map/own_1/pallas_call | solution.py:251
  132.4 2.2 %finish.1 = bf16[8,128,128]{2,1,0:T(8,128)(2,1)} custom-call(f32[1024,128]{1,0:T(8,128)} %copy-done.1, bf16[4,128,128]{2,1,0:T(8,128)(2,1)} %copy-done.21, bf16[4,128,128]{2,1,0:T(8,128)(2,1)} %copy-done.19, bf16[4,128,128]{2,1,0:T(8,128)(2,1)} %copy-done.20, bf16[4,128,128]{2,1,0:T(8,128)(2,1)} %copy-done.22, bf16[8,128,128]{2,1,0:T(8,128)(2,1)} %copy-done.18), custom_call_target="tpu_custom_call" | custom-call | tf_op jit(solution)/shard_map/finish/pallas_call | solution.py:286
  134.6 12.6 %all_to_all.10 = bf16[8,128,128]{2,1,0:T(8,128)(2,1)S(1)} all-to-all(bf16[8,128,128]{2,1,0:T(8,128)(2,1)} %finish.1), channel_id=1, replica_groups=mesh['y'=4,'xh'=2,'c'=2,'z'=4,'xl'=2] {'z','xl'}, dimensions={0} | all-to-all | bytes 524288 | tf_op jit(solution)/shard_map/all_to_all | solution.py:395
  147.9 3.0 %close.1 = (f32[1024,128]{1,0:T(8,128)}, f32[1024,128]{1,0:T(8,128)}, f32[128,128]{1,0:T(8,128)}, f32[128,128]{1,0:T(8,128)}) custom-call(f32[256,1152]{1,0:T(8,128)} %copy-done, f32[256,1152]{1,0:T(8,128)} %collective-permute-done.15.core, bf16[256,1152]{1,0:T(8,128)(2,1)} %collective-permute-done.16.chip), custom_call_target="tpu_custom_call" | custom-call | tf_op jit(solution)/shard_map/close/pallas_call | solution.py:305
  (81 shorter events, 17.1 us)
Async XLA Ops:
  6.9 19.2 %copy-start.23 = (f32[128,8]{0,1:T(8,128)S(1)}, f32[128,8]{0,1:T(8,128)}, u32[]{:S(2)}) copy-start(f32[128,8]{0,1:T(8,128)} %param.12) | copy-start | bytes 12292
  8.3 17.8 %collective-permute-start = (bf16[2304,128]{1,0:T(8,128)(2,1)S(1)}, bf16[2304,128]{1,0:T(8,128)(2,1)S(1)}, u32[]{:S(2)}, u32[]{:S(2)}) collective-permute-start(bf16[2304,128]{1,0:T(8,128)(2,1)S(1)} %get-tuple-element.47.refs_6_.refs_5_), channel_id=1, source_target_pairs={{0,16},{16,0},{1,17},{17,1},{2,18},{18,2},{3,19},{19,3},{4,20},{20... | collective-permute-start | bytes 1769480 | tf_op jit(solution)/shard_map/ppermute | solution.py:340
  11.5 34.2 %copy-start.17 = (s32[8]{0:T(128)S(1)}, s32[8]{0:T(128)}, u32[]{:S(2)}) copy-start(s32[8]{0:T(128)} %refs_1_.15) | copy-start | bytes 100
  11.5 27.4 %all-to-all-start = ((bf16[8,272,128]{2,1,0:T(8,128)(2,1)}), bf16[8,272,128]{2,1,0:T(8,128)(2,1)S(1)}, u32[]{:S(2)}, u32[]{:S(2)}) async-start(bf16[8,272,128]{2,1,0:T(8,128)(2,1)} %get-tuple-element.46), calls=%async_computation | async-start | bytes 1114112 | tf_op jit(solution)/shard_map/all_to_all | solution.py:343
  17.0 25.3 %collective-permute-start.2 = (bf16[2304,128]{1,0:T(8,128)(2,1)S(1)}, bf16[2304,128]{1,0:T(8,128)(2,1)S(1)}, u32[]{:S(2)}, u32[]{:S(2)}) collective-permute-start(bf16[2304,128]{1,0:T(8,128)(2,1)S(1)} %get-tuple-element.47.refs_6_.refs_5_), channel_id=1, source_target_pairs={{0,8},{8,0},{1,9},{9,1},{2,10},{10,2},{3,11},{11,3},{4,12},{12,4},... | collective-permute-start | bytes 1769480 | tf_op jit(solution)/shard_map/ppermute | solution.py:341
  26.1 18.7 %copy-start.11 = (bf16[2304,128]{1,0:T(8,128)(2,1)}, bf16[2304,128]{1,0:T(8,128)(2,1)S(1)}, u32[]{:S(2)}) copy-start(bf16[2304,128]{1,0:T(8,128)(2,1)S(1)} %collective-permute-done.refs_4_.refs_5_) | copy-start | bytes 1769476
  26.1 18.7 %collective-permute-start.1 = (bf16[2304,128]{1,0:T(8,128)(2,1)S(1)}, bf16[2304,128]{1,0:T(8,128)(2,1)S(1)}, u32[]{:S(2)}, u32[]{:S(2)}) collective-permute-start(bf16[2304,128]{1,0:T(8,128)(2,1)S(1)} %collective-permute-done.refs_4_.refs_5_), channel_id=1, source_target_pairs={{0,8},{8,0},{1,9},{9,1},{2,10},{10,2},{3,11},{11,3},{4,12},{12,4},... | collective-permute-start | bytes 1769480 | tf_op jit(solution)/shard_map/ppermute | solution.py:342
  38.9 18.8 %collective-permute-start.5 = (bf16[4,272,128]{2,1,0:T(8,128)(2,1)S(1)}, bf16[4,272,128]{2,1,0:T(8,128)(2,1)S(1)}, u32[]{:S(2)}, u32[]{:S(2)}) collective-permute-start(bf16[4,272,128]{2,1,0:T(8,128)(2,1)S(1)} %get-tuple-element.87), channel_id=1, source_target_pairs={{0,96},{32,0},{64,32},{96,64},{1,97},{33,1},{65,33},{97,65},{2,98}... | collective-permute-start | bytes 835592 | tf_op jit(solution)/shard_map/ppermute | solution.py:345
  41.5 26.3 %collective-permute-start.4 = (bf16[4,272,128]{2,1,0:T(8,128)(2,1)S(1)}, bf16[4,272,128]{2,1,0:T(8,128)(2,1)S(1)}, u32[]{:S(2)}, u32[]{:S(2)}) collective-permute-start(bf16[4,272,128]{2,1,0:T(8,128)(2,1)S(1)} %get-tuple-element.87), channel_id=1, source_target_pairs={{0,32},{32,64},{64,96},{96,0},{1,33},{33,65},{65,97},{97,1},{2,34}... | collective-permute-start | bytes 835592 | tf_op jit(solution)/shard_map/ppermute | solution.py:348
  41.5 16.3 %collective-permute-start.6 = (bf16[4,272,128]{2,1,0:T(8,128)(2,1)S(1)}, bf16[4,272,128]{2,1,0:T(8,128)(2,1)S(1)}, u32[]{:S(2)}, u32[]{:S(2)}) collective-permute-start(bf16[4,272,128]{2,1,0:T(8,128)(2,1)S(1)} %get-tuple-element.88), channel_id=1, source_target_pairs={{0,32},{32,64},{64,96},{96,0},{1,33},{33,65},{65,97},{97,1},{2,34}... | collective-permute-start | bytes 835592 | tf_op jit(solution)/shard_map/ppermute | solution.py:346
  42.3 15.4 %copy-start.9 = (bf16[2304,128]{1,0:T(8,128)(2,1)}, bf16[2304,128]{1,0:T(8,128)(2,1)S(1)}, u32[]{:S(2)}) copy-start(bf16[2304,128]{1,0:T(8,128)(2,1)S(1)} %collective-permute-done.2.refs_6_.refs_7_) | copy-start | bytes 1769476
  42.3 25.5 %collective-permute-start.3 = (bf16[4,272,128]{2,1,0:T(8,128)(2,1)S(1)}, bf16[4,272,128]{2,1,0:T(8,128)(2,1)S(1)}, u32[]{:S(2)}, u32[]{:S(2)}) collective-permute-start(bf16[4,272,128]{2,1,0:T(8,128)(2,1)S(1)} %get-tuple-element.88), channel_id=1, source_target_pairs={{0,96},{32,0},{64,32},{96,64},{1,97},{33,1},{65,33},{97,65},{2,98}... | collective-permute-start | bytes 835592 | tf_op jit(solution)/shard_map/ppermute | solution.py:347
  57.8 25.3 %collective-permute-start.7 = (bf16[4,272,128]{2,1,0:T(8,128)(2,1)S(1)}, bf16[4,272,128]{2,1,0:T(8,128)(2,1)S(1)}, u32[]{:S(2)}, u32[]{:S(2)}) collective-permute-start(bf16[4,272,128]{2,1,0:T(8,128)(2,1)S(1)} %collective-permute-done.5.refs_3_), channel_id=1, source_target_pairs={{0,96},{32,0},{64,32},{96,64},{1,97},{33,1},{65,33},{97,65},{2,98}... | collective-permute-start | bytes 835592 | tf_op jit(solution)/shard_map/ppermute | solution.py:357
  59.8 23.3 %collective-permute-start.8 = (bf16[4,272,128]{2,1,0:T(8,128)(2,1)S(1)}, bf16[4,272,128]{2,1,0:T(8,128)(2,1)S(1)}, u32[]{:S(2)}, u32[]{:S(2)}) collective-permute-start(bf16[4,272,128]{2,1,0:T(8,128)(2,1)S(1)} %collective-permute-done.6.refs_4_), channel_id=1, source_target_pairs={{0,32},{32,64},{64,96},{96,0},{1,33},{33,65},{65,97},{97,1},{2,34}... | collective-permute-start | bytes 835592 | tf_op jit(solution)/shard_map/ppermute | solution.py:358
  90.7 7.5 %collective-permute-start.9 = (f32[256,1152]{1,0:T(8,128)S(1)}, f32[256,1152]{1,0:T(8,128)S(1)}, u32[]{:S(2)}, u32[]{:S(2)}) collective-permute-start(f32[256,1152]{1,0:T(8,128)S(1)} %get-tuple-element.67), channel_id=1, source_target_pairs={{0,8},{8,0},{1,9},{9,1},{2,10},{10,2},{3,11},{11,3},{4,12},{12,4},... | collective-permute-start | bytes 3538952 | tf_op jit(solution)/shard_map/ppermute | solution.py:376
  106.7 41.3 %collective-permute-start.15 = (f32[256,1152]{1,0:T(8,128)S(1)}, f32[256,1152]{1,0:T(8,128)}, u32[]{:S(2)}, u32[]{:S(2)}) collective-permute-start(f32[256,1152]{1,0:T(8,128)S(1)} %get-tuple-element.82), channel_id=1, source_target_pairs={{0,8},{8,0},{1,9},{9,1},{2,10},{10,2},{3,11},{11,3},{4,12},{12,4},... | collective-permute-start | bytes 3538952 | tf_op jit(solution)/shard_map/ppermute | solution.py:389
  107.2 40.7 %collective-permute-start.16 = (bf16[256,1152]{1,0:T(8,128)(2,1)}, bf16[256,1152]{1,0:T(8,128)(2,1)}, u32[]{:S(2)}, u32[]{:S(2)}) collective-permute-start(bf16[256,1152]{1,0:T(8,128)(2,1)} %add_convert_fusion), channel_id=1, source_target_pairs={{0,16},{16,0},{1,17},{17,1},{2,18},{18,2},{3,19},{19,3},{4,20},{20... | collective-permute-start | bytes 1769480 | tf_op jit(solution)/shard_map/ppermute | solution.py:382
  110.8 5.2 %collective-permute-start.11 = (bf16[4,128,128]{2,1,0:T(8,128)(2,1)S(1)}, bf16[4,128,128]{2,1,0:T(8,128)(2,1)S(1)}, u32[]{:S(2)}, u32[]{:S(2)}) collective-permute-start(bf16[4,128,128]{2,1,0:T(8,128)(2,1)S(1)} %get-tuple-element.79), channel_id=1, source_target_pairs={{0,96},{32,0},{64,32},{96,64},{1,97},{33,1},{65,33},{97,65},{2,98}... | collective-permute-start | bytes 393224 | tf_op jit(solution)/shard_map/ppermute | solution.py:371
  112.5 11.8 %collective-permute-start.12 = (bf16[4,128,128]{2,1,0:T(8,128)(2,1)S(1)}, bf16[4,128,128]{2,1,0:T(8,128)(2,1)S(1)}, u32[]{:S(2)}, u32[]{:S(2)}) collective-permute-start(bf16[4,128,128]{2,1,0:T(8,128)(2,1)S(1)} %get-tuple-element.61), channel_id=1, source_target_pairs={{0,32},{32,64},{64,96},{96,0},{1,33},{33,65},{65,97},{97,1},{2,34}... | collective-permute-start | bytes 393224 | tf_op jit(solution)/shard_map/ppermute | solution.py:370
  112.8 18.2 %collective-permute-start.14 = (bf16[8,128,128]{2,1,0:T(8,128)(2,1)S(1)}, bf16[8,128,128]{2,1,0:T(8,128)(2,1)S(1)}, u32[]{:S(2)}, u32[]{:S(2)}) collective-permute-start(bf16[8,128,128]{2,1,0:T(8,128)(2,1)S(1)} %get-tuple-element.71), channel_id=1, source_target_pairs={{0,64},{32,96},{64,0},{96,32},{1,65},{33,97},{65,1},{97,33},{2,66}... | collective-permute-start | bytes 786440 | tf_op jit(solution)/shard_map/ppermute | solution.py:380
  116.0 8.2 %copy-start.19 = (bf16[4,128,128]{2,1,0:T(8,128)(2,1)}, bf16[4,128,128]{2,1,0:T(8,128)(2,1)S(1)}, u32[]{:S(2)}) copy-start(bf16[4,128,128]{2,1,0:T(8,128)(2,1)S(1)} %collective-permute-done.11.up_b) | copy-start | bytes 393220
  116.0 15.0 %collective-permute-start.10 = (bf16[4,128,128]{2,1,0:T(8,128)(2,1)S(1)}, bf16[4,128,128]{2,1,0:T(8,128)(2,1)S(1)}, u32[]{:S(2)}, u32[]{:S(2)}) collective-permute-start(bf16[4,128,128]{2,1,0:T(8,128)(2,1)S(1)} %get-tuple-element.78), channel_id=1, source_target_pairs={{0,96},{32,0},{64,32},{96,64},{1,97},{33,1},{65,33},{97,65},{2,98}... | collective-permute-start | bytes 393224 | tf_op jit(solution)/shard_map/ppermute | solution.py:388
  124.2 6.7 %collective-permute-start.13 = (bf16[4,128,128]{2,1,0:T(8,128)(2,1)S(1)}, bf16[4,128,128]{2,1,0:T(8,128)(2,1)S(1)}, u32[]{:S(2)}, u32[]{:S(2)}) collective-permute-start(bf16[4,128,128]{2,1,0:T(8,128)(2,1)S(1)} %get-tuple-element.80), channel_id=1, source_target_pairs={{0,32},{32,64},{64,96},{96,0},{1,33},{33,65},{65,97},{97,1},{2,34}... | collective-permute-start | bytes 393224 | tf_op jit(solution)/shard_map/ppermute | solution.py:387
  130.9 17.0 %copy-start = (f32[256,1152]{1,0:T(8,128)}, f32[256,1152]{1,0:T(8,128)S(1)}, u32[]{:S(2)}) copy-start(f32[256,1152]{1,0:T(8,128)S(1)} %get-tuple-element.81.own) | copy-start | bytes 3538948
  (18 other events, 36.0 us)

commit v2 on v1

v2 whole, which is shorter than its diff:
```python
import functools

import jax
import jax.numpy as jnp
from jax import lax
from jax.experimental import pallas as pl
from jax.experimental.pallas import tpu as pltpu
from jax.sharding import Mesh
from jax.sharding import PartitionSpec as P

F32 = jnp.float32
BF16 = jnp.bfloat16
HD = 128
GROUP = 8
BLOCK = 128
NBLK = 16
PK = 1024
RK = 128
KW = PK + RK
QR = BLOCK * GROUP
SRC = 8
SUB = BLOCK // SRC
DROW = 2 * BLOCK
LROW = DROW + 8
PAY = LROW + 8
SCALE = HD ** (-0.5)
LOG2E = 1.4426950408889634
C2 = SCALE * LOG2E

NN = (((1,), (0,)), ((), ()))
NT = (((1,), (1,)), ((), ()))

Y, XH, C, Z, XL = "y", "xh", "c", "z", "xl"
BULK = (Z, XL)


def dot(a, b, dims):
    return lax.dot_general(a, b, dims, preferred_element_type=F32)


def held(*arrays):
    return [pltpu.with_memory_space_constraint(a, pltpu.VMEM) for a in arrays]


ANYSPEC = pl.BlockSpec(memory_space=pl.ANY)
VSPEC = pl.BlockSpec(memory_space=pltpu.VMEM)
SSPEC = pl.BlockSpec(memory_space=pltpu.SMEM)


def pieces_of(x):
    a = x.astype(BF16).astype(F32)
    b = (x - a).astype(BF16).astype(F32)
    return a, b, x - a - b


def pack_kernel(q_in, g_in, o_in, pk, rk, pv, rv, pay, kv, q, g, o, sems):
    loads = [
        pltpu.make_async_copy(src, dst, sems.at[n])
        for n, (src, dst) in enumerate(((q_in, q), (g_in, g), (o_in, o)))
    ]
    copies, at = [], 0
    for n, (src, rows) in enumerate(((pk, PK), (rk, RK), (pv, PK), (rv, RK))):
        copies.append(pltpu.make_async_copy(src, kv.at[pl.ds(at, rows)], sems.at[3 + n]))
        at += rows
    for copy in loads + copies:
        copy.start()
    for copy in loads:
        copy.wait()
    ones = jnp.ones((16, HD), BF16)
    row = lax.broadcasted_iota(jnp.int32, (16, BLOCK), 0)
    for b in range(SRC):
        prods = []
        for h in range(GROUP):
            cols = slice((b * GROUP + h) * HD, (b * GROUP + h + 1) * HD)
            qh, gh = q[:, cols], g[:, cols]
            pay[b, h * SUB : (h + 1) * SUB, :] = qh
            pay[b, BLOCK + h * SUB : BLOCK + (h + 1) * SUB, :] = gh
            prods.append(gh.astype(F32) * o[:, cols].astype(F32))
        prod = jnp.concatenate(prods, axis=0)
        high = prod.astype(BF16)
        low = (prod - high.astype(F32)).astype(BF16)
        d1, d2, d3 = pieces_of(dot(ones, high, NT) + dot(ones, low, NT))
        rows = jnp.where(row == 0, d1, jnp.where(row == 1, d2, jnp.where(row == 2, d3, 0.0)))
        pay[b, DROW:PAY, :] = rows.astype(BF16)
    for copy in copies:
        copy.wait()


def pack(*arrays):
    arrays = [pltpu.with_memory_space_constraint(a, pltpu.HBM) for a in arrays]
    return pl.pallas_call(
        pack_kernel,
        in_specs=[ANYSPEC] * 7,
        out_specs=[VSPEC, VSPEC],
        out_shape=[pltpu.VMEM((SRC, PAY, HD), BF16), pltpu.VMEM((2 * KW, HD), BF16)],
        scratch_shapes=[pltpu.VMEM((SUB, SRC * GROUP * HD), BF16)] * 3
        + [pltpu.SemaphoreType.DMA((7,))],
        compiler_params=pltpu.CompilerParams(vmem_limit_bytes=16 << 20),
        name="pack",
    )(*arrays)


def column(rows):
    line = jnp.concatenate([rows[s : s + 1, :] for s in range(SRC)], axis=1)
    return jnp.broadcast_to(line, (HD, QR)).T


def tiles_kernel(cfg, *refs):
    unit, far, first, last, more_g, more_dq, final = cfg
    refs = list(refs)

    def take(n):
        out = refs[:n]
        del refs[:n]
        return out

    place, lengths = take(2)
    pays = take(1 if unit == "own" else 2)
    key_in = take(last - first)
    take(1 if more_g else 0)
    dq_in = take(1 if more_dq else 0)
    sums = take(1)[0]
    split = final and unit in ("near_a", "near_b")
    dq_out = take(2 if split else 1)
    qs, gs, qt, gt, keys, log_col, delta_col, dqa = refs

    rows = QR // len(pays)
    scalars = []
    for n, pay in enumerate(pays):
        qs[n * rows : (n + 1) * rows, :] = pay[:, 0:BLOCK, :].reshape(rows, HD)
        gs[n * rows : (n + 1) * rows, :] = pay[:, BLOCK : 2 * BLOCK, :].reshape(rows, HD)
        scalars.append(pay[:, DROW:PAY, :].astype(F32))
    scalars = jnp.concatenate(scalars, axis=0)
    add = lambda n: scalars[:, n, :] + scalars[:, n + 1, :] + scalars[:, n + 2, :]
    delta_col[...] = column(add(0))
    log_col[...] = column(add(LROW - DROW))
    qt[...] = qs[...].T
    gt[...] = gs[...].T
    if more_dq:
        dqa[...] = dq_in[0][...]
    else:
        dqa[...] = jnp.zeros((QR, HD), F32)
    y, xh, c = place[0], place[1], place[2]

    def step(j, carry):
        for n in range(first, last):

            @pl.when(j == n)
            def _():
                keys[...] = key_in[n - first][...]

        def products(at, width, rows):
            s = dot(qs[:rows], keys[at : at + width, :], NT)
            dp = dot(gs[:rows], keys[KW + at : KW + at + width, :], NT)
            return s, dp

        def grads(at, width, rows, s, dp, allowed):
            wide = lambda col: jnp.concatenate([col[:rows]] * (width // HD), axis=1)
            p = jnp.exp2(s * C2 - wide(log_col))
            if allowed is not None:
                p = jnp.where(allowed, p, 0.0)
            ds = (p * (dp - wide(delta_col))).astype(BF16)
            p = p.astype(BF16)
            dk = dot(qt[:, :rows], ds, NN)
            dv = dot(gt[:, :rows], p, NN)
            cols = slice(at, at + width)
            if more_g or at >= PK:
                sums[j, 0:HD, cols] += dk
                sums[j, HD : 2 * HD, cols] += dv
            else:
                sums[j, 0:HD, cols] = dk
                sums[j, HD : 2 * HD, cols] = dv
            return dot(ds, keys[at : at + width, :], NN)

        if not more_g:
            sums[j, :, PK:KW] = jnp.zeros((2 * HD, RK), F32)
        part = 256
        total = None
        ahead = products(0, part, QR)
        for n in range(PK // part):
            s, dp = ahead
            if n + 1 < PK // part:
                ahead = products((n + 1) * part, part, QR)
            term = grads(n * part, part, QR, s, dp, None)
            total = term if total is None else total + term
        dqa[...] += total

        if unit != "opp":
            rows = QR if unit == "own" else QR // 2
            qi = 4 * (y if unit == "own" else (y + 1) % 4) + 2 * xh + c
            kj = 4 * y + 2 * ((1 - xh) if far else xh) + (c + j - 2 * c * j)
            seen, end = kj <= qi, 0
            for r in range(lengths.shape[0]):
                end = end + lengths[r]
                seen = seen & ((end <= kj) | (end > qi))

            @pl.when(seen)
            def _():
                allowed = None
                if unit == "own":
                    row = lax.broadcasted_iota(jnp.int32, (rows, RK), 0)
                    key_at = lax.broadcasted_iota(jnp.int32, (rows, RK), 1)
                    token = (row // BLOCK) * SUB + row % SUB
                    allowed = (kj < qi) | (key_at <= token)
                s, dp = products(PK, RK, rows)
                dqa[:rows, :] += grads(PK, RK, rows, s, dp, allowed)

        return carry

    lax.fori_loop(first, last, step, 0)
    if not more_g and last - first < 2:
        sums[1 - first] = jnp.zeros((2 * HD, KW), F32)
    if final and unit != "own":
        done = (dqa[...] * SCALE).astype(BF16).reshape(SRC, BLOCK, HD)
        if split:
            dq_out[0][...], dq_out[1][...] = done[0:4], done[4:8]
        else:
            dq_out[0][...] = done
    else:
        dq_out[0][...] = dqa[...]


def tiles(name, place, lengths, pays, keys, sums=None, dq=None, final=False):
    unit, where = name.rsplit("_", 1)
    first, last = {"mine": (0, 1), "core": (1, 2)}.get(where, (0, 2))
    cfg = (unit, where == "far", first, last, sums is not None, dq is not None, final)
    operands = held(*pays, *keys)
    aliases = {}
    if sums is not None:
        aliases[2 + len(operands)] = 0
        operands += held(sums)
    if dq is not None:
        if not final or unit == "own":
            aliases[2 + len(operands)] = 1
        operands += held(dq)
    if not final or unit == "own":
        dq_shapes = [pltpu.VMEM((QR, HD), F32)]
    elif unit == "opp":
        dq_shapes = [pltpu.VMEM((SRC, BLOCK, HD), BF16)]
    else:
        dq_shapes = [pltpu.VMEM((SRC // 2, BLOCK, HD), BF16)] * 2
    sums, *dqs = pl.pallas_call(
        functools.partial(tiles_kernel, cfg),
        in_specs=[SSPEC] * 2 + [VSPEC] * len(operands),
        out_specs=[VSPEC] * (1 + len(dq_shapes)),
        out_shape=[pltpu.VMEM((2, 2 * HD, KW), F32)] + dq_shapes,
        scratch_shapes=[
            pltpu.VMEM((QR, HD), BF16),
            pltpu.VMEM((QR, HD), BF16),
            pltpu.VMEM((HD, QR), BF16),
            pltpu.VMEM((HD, QR), BF16),
            pltpu.VMEM((2 * KW, HD), BF16),
            pltpu.VMEM((QR, HD), F32),
            pltpu.VMEM((QR, HD), F32),
            pltpu.VMEM((QR, HD), F32),
        ],
        input_output_aliases=aliases,
        compiler_params=pltpu.CompilerParams(vmem_limit_bytes=24 << 20),
        cost_estimate=pl.CostEstimate(
            flops=QR * PK * HD, bytes_accessed=1 << 18, transcendentals=0
        ),
        name=name,
    )(place, lengths, *operands)
    return sums, (dqs[0] if len(dqs) == 1 else dqs)


def finish_kernel(own, up_a, up_b, down_a, down_b, opp, out):
    for s in range(SRC):
        up, down = (up_a, down_a) if s < 4 else (up_b, down_b)
        rows = own[s * BLOCK : (s + 1) * BLOCK, :] * SCALE
        rows = rows + up[s % 4].astype(F32) + down[s % 4].astype(F32) + opp[s].astype(F32)
        out[s] = rows.astype(BF16)


def finish(*terms):
    return pl.pallas_call(
        finish_kernel,
        in_specs=[VSPEC] * 6,
        out_specs=VSPEC,
        out_shape=pltpu.VMEM((SRC, BLOCK, HD), BF16),
        name="finish",
    )(*held(*terms))


def close_kernel(own, core, chip, dk, dv, drk, drv):
    def total(rows, cols):
        part = own[0, rows, cols] + core[rows, cols] + chip[rows, cols].astype(F32)
        return part.T

    keys, values = slice(0, HD), slice(HD, 2 * HD)
    dk[...] = total(keys, slice(0, PK)) * SCALE
    drk[...] = total(keys, slice(PK, KW)) * SCALE
    dv[...] = total(values, slice(0, PK))
    drv[...] = total(values, slice(PK, KW))


def close(own, core, chip):
    shape = lambda rows: jax.ShapeDtypeStruct((rows, HD), F32)
    return pl.pallas_call(
        close_kernel,
        in_specs=[VSPEC] * 3,
        out_specs=[VSPEC] * 4,
        out_shape=[shape(PK), shape(PK), shape(RK), shape(RK)],
        compiler_params=pltpu.CompilerParams(vmem_limit_bytes=16 << 20),
        name="close",
    )(*held(own, core, chip))


def shift(n, s):
    return [(i, (i + s) % n) for i in range(n)]


def after(values, *earlier):
    return lax.optimization_barrier((values, earlier))[0]


def shards(
    queries,
    out_grad,
    attn_out,
    log_totals,
    prompt_keys,
    prompt_values,
    rollout_keys,
    rollout_values,
    rollout_blocks,
):
    place = jnp.stack([lax.axis_index(Y), lax.axis_index(XH), lax.axis_index(C)])
    place = place.astype(jnp.int32)
    to_next, to_last, swap = shift(4, 1), shift(4, -1), shift(2, 1)

    logs = (log_totals * LOG2E).reshape(SRC, SUB, GROUP).transpose(0, 2, 1).reshape(SRC, 1, BLOCK)
    l1 = lax.reduce_precision(logs, 8, 7)
    l2 = lax.reduce_precision(logs - l1, 8, 7)
    logs = [p.astype(BF16) for p in (l1, l2, logs - l1 - l2)]
    logs = jnp.concatenate(logs + [jnp.zeros((SRC, PAY - LROW - 3, BLOCK), BF16)], axis=1)

    payload, kv_own = pack(
        queries, out_grad, attn_out, prompt_keys, rollout_keys, prompt_values, rollout_values
    )
    kv_x = lax.ppermute(kv_own, XH, swap)
    kv_c = lax.ppermute(kv_own, C, swap)
    own = lax.all_to_all(payload, BULK, split_axis=0, concat_axis=0, tiled=True)
    kv_xc = lax.ppermute(kv_x, C, swap)
    own = own.at[:, LROW:PAY, :].set(logs)
    own_a, own_b = own[:4], own[4:]
    up_a = lax.ppermute(own_a, Y, to_last)
    down_b = lax.ppermute(own_b, Y, to_next)
    up_b = lax.ppermute(own_b, Y, to_last)
    down_a = lax.ppermute(own_a, Y, to_next)

    run = lambda name, *rest: tiles(name, place, rollout_blocks, *rest)
    far, here = [kv_x, kv_xc], [kv_own, kv_c]
    g_far, dq_own = run("own_far", [own], far)
    g_here, dq_own = run("own_core", [own], here[1:], None, dq_own)
    up_a, down_b = after((up_a, down_b), dq_own)
    opp_a = lax.ppermute(up_a, Y, to_last)
    opp_b = lax.ppermute(down_b, Y, to_next)
    g_far, dq_a = run("near_a_far", [up_a, down_b], far, g_far)
    up_b, down_a = after((up_b, down_a), dq_a)
    g_far, dq_b = run("near_b_far", [up_b, down_a], far, g_far)
    dq_a = after(dq_a, dq_b)
    g_here, (a_up, a_down) = run("near_a_here", [up_a, down_b], here, g_here, dq_a, True)
    from_a_down = lax.ppermute(a_up, Y, to_next)
    from_a_up = lax.ppermute(a_down, Y, to_last)
    opp_a, opp_b = after((opp_a, opp_b), a_up)
    g_far, dq_opp = run("opp_far", [opp_a, opp_b], far, g_far)
    from_core = lax.ppermute(g_far[1], C, swap)
    g_here, opp = run("opp_here", [opp_a, opp_b], here, g_here, dq_opp, True)
    from_opp = lax.ppermute(opp, Y, shift(4, 2))
    to_chip = (g_far[0] + after(from_core, opp)).astype(BF16)
    from_chip = lax.ppermute(to_chip, XH, swap)
    dq_b = after(dq_b, to_chip, from_a_down, from_a_up)
    g_here, (b_up, b_down) = run("near_b_here", [up_b, down_a], here, g_here, dq_b, True)
    from_b_down = lax.ppermute(b_up, Y, to_next)
    from_b_up = lax.ppermute(b_down, Y, to_last)
    from_c = lax.ppermute(g_here[1], C, swap)
    dq_own = after(dq_own, b_up)
    g_here, dq_own = run("own_mine", [own], here[:1], g_here, dq_own, True)
    dk, dv, drk, drv = close(g_here, from_c, from_chip)
    dq_own = after(dq_own, drk)

    dq = finish(dq_own, from_b_up, from_a_up, from_a_down, from_b_down, from_opp)
    dq = lax.all_to_all(dq, BULK, split_axis=0, concat_axis=0, tiled=True)
    query_grad = dq.reshape(SRC * GROUP, SUB, HD).transpose(1, 0, 2).reshape(SUB, SRC * GROUP * HD)
    return (query_grad, dk, dv, drk, drv)


def solution(mesh):
    fine = Mesh(mesh.devices.reshape(4, 2, 2, 4, 2), (Y, XH, C, Z, XL))
    hold, bulk = (Y, XH, C), (Z, XL)
    tokens = P(hold + bulk, None)
    split = P(hold, bulk)
    return jax.shard_map(
        shards,
        mesh=fine,
        in_specs=(tokens, tokens, tokens, split, split, split, split, split, P()),
        out_specs=(tokens, split, split, split, split),
        check_vma=False,
    )
```

time: 152 us -> 124 us (0.82)
  blocking collectives: 25.1 us -> 9.77 us
  Pallas kernels: 67.3 us -> 54.9 us
  waiting for transfers between devices: 16.6 us -> 25.5 us
  local copies, waits for them, and re-layouts: 13 us -> 5.07 us
    all_gather x1 -> x0, blocking collectives: 12.5 us -> none  [shards(): l_all = lax.all_gather(l0, Y, axis=0, tiled=False)]
    pallas_call x11 -> x12, Pallas kernels: 67.3 us -> 54.9 us  [the longest x9 51 us: tiles(): pl.pallas_call(functools.partial(tiles_kernel, cfg), in_specs=[SSPEC] * 2...]
    unnamed x48 -> x12, local copies, waits for them, and re-layouts: 12.1 us -> 3.11 us
    all_to_all x1, waiting for transfers between devices: 0.01 us -> 8.44 us  [shards(): own = lax.all_to_all(payload, BULK, split_axis=0, concat_axis=0, tiled=True)]
    ppermute x1, waiting for transfers between devices: 0.01 us -> 8.01 us  [shards(): from_chip = lax.ppermute(to_chip, XH, swap)]
    ppermute x1, waiting for transfers between devices: 5.34 us -> 0.01 us  [shards(): from_a_down = lax.ppermute(a_up, Y, to_next)]
    all_to_all x1, blocking collectives: 12.6 us -> 9.77 us  [shards(): dq = lax.all_to_all(dq, BULK, split_axis=0, concat_axis=0, tiled=True)]
    ppermute x1, starting transfers between devices: 2.9 us -> 0.49 us  [shards(): from_b_up = lax.ppermute(b_down, Y, to_last)]
  transfers between devices with their start and end apart: 18 -> 18, of which waited for: 3 -> 3; matrix products, arithmetic and copies ran while one was open for 1% -> 1% of each run, Pallas kernels for 32% -> 33%
where the time goes in v2:
time: 124 us
  Pallas kernels  54.9 us (44%)
  starting transfers between devices  27.2 us (22%)
  waiting for transfers between devices  25.5 us (21%)
  blocking collectives  9.77 us (8%)
  local copies, waits for them, and re-layouts  5.07 us (4%)
    pallas_call x9, Pallas kernels, tiles(): pl.pallas_call(functools.partial(tiles_kernel, cfg), in_specs=[SSPEC] * 2...  51 us
    all_to_all x1, blocking collectives, shards(): dq = lax.all_to_all(dq, BULK, split_axis=0, concat_axis=0, tiled=True)  9.77 us
    ppermute x1, waiting for transfers between devices, shards(): kv_x = lax.ppermute(kv_own, XH, swap)  8.99 us
    all_to_all x1, waiting for transfers between devices, shards(): own = lax.all_to_all(payload, BULK, split_axis=0, concat_axis=0, tiled=True)  8.44 us
    ppermute x1, waiting for transfers between devices, shards(): from_chip = lax.ppermute(to_chip, XH, swap)  8.01 us
    all_to_all x1, starting transfers between devices, shards(): own = lax.all_to_all(payload, BULK, split_axis=0, concat_axis=0, tiled=True)  5.34 us
    ppermute x1, starting transfers between devices, shards(): opp_a = lax.ppermute(up_a, Y, to_last)  3.31 us
    ppermute x1, starting transfers between devices, shards(): up_b = lax.ppermute(own_b, Y, to_last)  3.23 us
  transfers between devices with their start and end apart: 18, of which 3 were waited for; matrix products, arithmetic and copies ran while one was open for 1% of the time, Pallas kernels for 33%

profile of v2, /device:TPU:0, one launch (start us, length us, event | category | flops | bytes accessed | tf_op | source)
XLA Modules:
  0.0 123.6 jit_solution(151515776777621585)
XLA Ops:
  0.7 2.4 %pack.1 = (bf16[8,272,128]{2,1,0:T(8,128)(2,1)}, bf16[2304,128]{1,0:T(8,128)(2,1)S(1)}) custom-call(bf16[16,8192]{1,0:T(8,128)(2,1)} %q_in.1, bf16[16,8192]{1,0:T(8,128)(2,1)} %g_in.1, bf16[16,8192]{1,0:T(8,128)(2,1)} %o_in.1, bf16[1024,128]{1,0:T(8,128)(2,1)} %pk.1, bf16[128,128]{1,0:T(8,128)(2,1)} %rk.1, bf16[1024,128]{1,0:T(8,128)(2,1)} %pv.1, ...), custom_call_target="tpu_custom_call" | custom-call | tf_op jit(solution)/shard_map/pack/pallas_call | solution.py:91
  3.1 3.2 %collective-permute-start.5 = (bf16[2304,128]{1,0:T(8,128)(2,1)S(1)}, bf16[2304,128]{1,0:T(8,128)(2,1)S(1)}, u32[]{:S(2)}, u32[]{:S(2)}) collective-permute-start(bf16[2304,128]{1,0:T(8,128)(2,1)S(1)} %get-tuple-element.55.refs_4_.refs_3_), channel_id=1, source_target_pairs={{0,16},{16,0},{1,17},{17,1},{2,18},{18,2},{3,19},{19,3},{4,20},{20... | collective-permute-start | bytes 1769480 | tf_op jit(solution)/shard_map/ppermute | solution.py:341
  6.3 5.3 %all-to-all-start = ((bf16[8,272,128]{2,1,0:T(8,128)(2,1)}), bf16[8,272,128]{2,1,0:T(8,128)(2,1)S(1)}, u32[]{:S(2)}, u32[]{:S(2)}) async-start(bf16[8,272,128]{2,1,0:T(8,128)(2,1)} %get-tuple-element.54), calls=%async_computation | async-start | bytes 1114112 | tf_op jit(solution)/shard_map/all_to_all | solution.py:343
  11.9 9.0 %collective-permute-done.5.refs_3_.refs_4_ = bf16[2304,128]{1,0:T(8,128)(2,1)S(1)} collective-permute-done((bf16[2304,128]{1,0:T(8,128)(2,1)S(1)}, bf16[2304,128]{1,0:T(8,128)(2,1)S(1)}, u32[]{:S(2)}, u32[]{:S(2)}) %collective-permute-start.5) | collective-permute-done | bytes 589856 | tf_op jit(solution)/shard_map/ppermute | solution.py:341
  20.9 8.4 %all-to-all-done = bf16[8,272,128]{2,1,0:T(8,128)(2,1)S(1)} async-done(((bf16[8,272,128]{2,1,0:T(8,128)(2,1)}), bf16[8,272,128]{2,1,0:T(8,128)(2,1)S(1)}, u32[]{:S(2)}, u32[]{:S(2)}) %all-to-all-start) | async-done | bytes 557088 | tf_op jit(solution)/shard_map/all_to_all | solution.py:343
  30.3 3.0 %collective-permute-start.2 = (bf16[4,272,128]{2,1,0:T(8,128)(2,1)}, bf16[4,272,128]{2,1,0:T(8,128)(2,1)}, u32[]{:S(2)}, u32[]{:S(2)}) collective-permute-start(bf16[4,272,128]{2,1,0:T(8,128)(2,1)} %get-tuple-element.91), channel_id=1, source_target_pairs={{0,96},{32,0},{64,32},{96,64},{1,97},{33,1},{65,33},{97,65},{2,98}... | collective-permute-start | bytes 835592 | tf_op jit(solution)/shard_map/ppermute | solution.py:347
  33.3 3.2 %collective-permute-start = (bf16[4,272,128]{2,1,0:T(8,128)(2,1)}, bf16[4,272,128]{2,1,0:T(8,128)(2,1)S(1)}, u32[]{:S(2)}, u32[]{:S(2)}) collective-permute-start(bf16[4,272,128]{2,1,0:T(8,128)(2,1)} %get-tuple-element.92), channel_id=1, source_target_pairs={{0,96},{32,0},{64,32},{96,64},{1,97},{33,1},{65,33},{97,65},{2,98}... | collective-permute-start | bytes 835592 | tf_op jit(solution)/shard_map/ppermute | solution.py:349
  36.6 5.9 %own_far.1 = (f32[2,256,1152]{2,1,0:T(8,128)S(1)}, f32[1024,128]{1,0:T(8,128)S(1)}) custom-call(s32[3]{0:T(128)S(1)} %pad_add_fusion.refs_0_, s32[8]{0:T(128)S(1)} %copy-done.4, bf16[8,272,128]{2,1,0:T(8,128)(2,1)S(1)} %maximum_dynamic-update-slice_fusion.refs_2_, bf16[2304,128]{1,0:T(8,128)(2,1)S(1)} %collective-permute-done.5.refs_3_.refs_4_, ...), custom_call_target="tpu_custom_call" | custom-call | flops 134217728 | bytes 262144 | tf_op jit(solution)/shard_map/own_far/pallas_call | solution.py:242
  42.6 3.2 %own_core.1 = (f32[2,256,1152]{2,1,0:T(8,128)S(1)}, f32[1024,128]{1,0:T(8,128)S(1)}) custom-call(s32[3]{0:T(128)S(1)} %pad_add_fusion.refs_0_, s32[8]{0:T(128)S(1)} %copy-done.4, bf16[8,272,128]{2,1,0:T(8,128)(2,1)S(1)} %maximum_dynamic-update-slice_fusion.refs_2_, ...), custom_call_target="tpu_custom_call", output_to_operand_aliasing={{1}: (4, {})} | custom-call | flops 134217728 | bytes 262144 | tf_op jit(solution)/shard_map/own_core/pallas_call | solution.py:242
  45.8 3.3 %collective-permute-start.7 = (bf16[4,272,128]{2,1,0:T(8,128)(2,1)}, bf16[4,272,128]{2,1,0:T(8,128)(2,1)S(1)}, u32[]{:S(2)}, u32[]{:S(2)}) collective-permute-start(bf16[4,272,128]{2,1,0:T(8,128)(2,1)} %collective-permute-done.2.refs_2_), channel_id=1, source_target_pairs={{0,96},{32,0},{64,32},{96,64},{1,97},{33,1},{65,33},{97,65},{2,98}... | collective-permute-start | bytes 835592 | tf_op jit(solution)/shard_map/ppermute | solution.py:357
  49.1 7.2 %near_a_far.1 = (f32[2,256,1152]{2,1,0:T(8,128)S(1)}, f32[1024,128]{1,0:T(8,128)S(1)}) custom-call(s32[3]{0:T(128)S(1)} %pad_add_fusion.refs_0_, s32[8]{0:T(128)S(1)} %copy-done.4, bf16[4,272,128]{2,1,0:T(8,128)(2,1)} %collective-permute-done.2.refs_2_, bf16[4,272,128]{2,1,0:T(8,128)(2,1)} %collective-permute-done.3.refs_3_, ...), custom_call_target="tpu_custom_call", output_to_operand_aliasing={{0}: (6, {})} | custom-call | flops 134217728 | bytes 262144 | tf_op jit(solution)/shard_map/near_a_far/pallas_call | solution.py:242
  56.3 6.5 %near_b_far.1 = (f32[2,256,1152]{2,1,0:T(8,128)S(1)}, f32[1024,128]{1,0:T(8,128)S(1)}) custom-call(s32[3]{0:T(128)S(1)} %pad_add_fusion.refs_0_, s32[8]{0:T(128)S(1)} %copy-done.4, bf16[4,272,128]{2,1,0:T(8,128)(2,1)S(1)} %collective-permute-done.refs_2_, bf16[4,272,128]{2,1,0:T(8,128)(2,1)S(1)} %collective-permute-done.1.refs_3_, ...), custom_call_target="tpu_custom_call", output_to_operand_aliasing={{0}: (6, {})} | custom-call | flops 134217728 | bytes 262144 | tf_op jit(solution)/shard_map/near_b_far/pallas_call | solution.py:242
  62.8 6.5 %near_a_here.1 = (f32[2,256,1152]{2,1,0:T(8,128)S(1)}, bf16[4,128,128]{2,1,0:T(8,128)(2,1)S(1)}, bf16[4,128,128]{2,1,0:T(8,128)(2,1)S(1)}) custom-call(s32[3]{0:T(128)S(1)} %pad_add_fusion.refs_0_, s32[8]{0:T(128)S(1)} %copy-done.4, bf16[4,272,128]{2,1,0:T(8,128)(2,1)} %collective-permute-done.2.refs_2_, ...), custom_call_target="tpu_custom_call", output_to_operand_aliasing={{0}: (6, {})} | custom-call | flops 134217728 | bytes 262144 | tf_op jit(solution)/shard_map/near_a_here/pallas_call | solution.py:242
  69.3 6.0 %opp_far.1 = (f32[2,256,1152]{2,1,0:T(8,128)S(1)}, f32[1024,128]{1,0:T(8,128)S(1)}) custom-call(s32[3]{0:T(128)S(1)} %pad_add_fusion.refs_0_, s32[8]{0:T(128)S(1)} %copy-done.4, bf16[4,272,128]{2,1,0:T(8,128)(2,1)S(1)} %collective-permute-done.7.refs_2_, bf16[4,272,128]{2,1,0:T(8,128)(2,1)S(1)} %collective-permute-done.8.refs_3_, ...), custom_call_target="tpu_custom_call", output_to_operand_aliasing={{0}: (6, {})} | custom-call | flops 134217728 | bytes 262144 | tf_op jit(solution)/shard_map/opp_far/pallas_call | solution.py:242
  75.7 3.2 %collective-permute-start.11 = (bf16[4,128,128]{2,1,0:T(8,128)(2,1)S(1)}, bf16[4,128,128]{2,1,0:T(8,128)(2,1)S(1)}, u32[]{:S(2)}, u32[]{:S(2)}) collective-permute-start(bf16[4,128,128]{2,1,0:T(8,128)(2,1)S(1)} %get-tuple-element.78), channel_id=1, source_target_pairs={{0,96},{32,0},{64,32},{96,64},{1,97},{33,1},{65,33},{97,65},{2,98}... | collective-permute-start | bytes 393224 | tf_op jit(solution)/shard_map/ppermute | solution.py:365
  79.0 6.0 %opp_here.1 = (f32[2,256,1152]{2,1,0:T(8,128)S(1)}, bf16[8,128,128]{2,1,0:T(8,128)(2,1)S(1)}) custom-call(s32[3]{0:T(128)S(1)} %pad_add_fusion.refs_0_, s32[8]{0:T(128)S(1)} %copy-done.4, bf16[4,272,128]{2,1,0:T(8,128)(2,1)S(1)} %collective-permute-done.7.refs_2_, ...), custom_call_target="tpu_custom_call", output_to_operand_aliasing={{0}: (6, {})} | custom-call | flops 134217728 | bytes 262144 | tf_op jit(solution)/shard_map/opp_here/pallas_call | solution.py:242
  85.1 6.0 %near_b_here.1 = (f32[2,256,1152]{2,1,0:T(8,128)S(1)}, bf16[4,128,128]{2,1,0:T(8,128)(2,1)S(1)}, bf16[4,128,128]{2,1,0:T(8,128)(2,1)S(1)}) custom-call(s32[3]{0:T(128)S(1)} %pad_add_fusion.refs_0_, s32[8]{0:T(128)S(1)} %copy-done.4, bf16[4,272,128]{2,1,0:T(8,128)(2,1)S(1)} %collective-permute-done.refs_2_, ...), custom_call_target="tpu_custom_call", output_to_operand_aliasing={{0}: (6, {})} | custom-call | flops 134217728 | bytes 262144 | tf_op jit(solution)/shard_map/near_b_here/pallas_call | solution.py:242
  91.3 1.9 %collective-permute-start.13 = (bf16[256,1152]{1,0:T(8,128)(2,1)S(1)}, bf16[256,1152]{1,0:T(8,128)(2,1)S(1)}, u32[]{:S(2)}, u32[]{:S(2)}) collective-permute-start(bf16[256,1152]{1,0:T(8,128)(2,1)S(1)} %fusion), channel_id=1, source_target_pairs={{0,16},{16,0},{1,17},{17,1},{2,18},{18,2},{3,19},{19,3},{4,20},{20... | collective-permute-start | bytes 1769480 | tf_op jit(solution)/shard_map/ppermute | solution.py:372
  93.2 1.5 %collective-permute-start.16 = (bf16[8,128,128]{2,1,0:T(8,128)(2,1)S(1)}, bf16[8,128,128]{2,1,0:T(8,128)(2,1)S(1)}, u32[]{:S(2)}, u32[]{:S(2)}) collective-permute-start(bf16[8,128,128]{2,1,0:T(8,128)(2,1)S(1)} %get-tuple-element.76), channel_id=1, source_target_pairs={{0,64},{32,96},{64,0},{96,32},{1,65},{33,97},{65,1},{97,33},{2,66}... | collective-permute-start | bytes 786440 | tf_op jit(solution)/shard_map/ppermute | solution.py:370
  95.1 1.5 %collective-permute-start.15 = (bf16[4,128,128]{2,1,0:T(8,128)(2,1)S(1)}, bf16[4,128,128]{2,1,0:T(8,128)(2,1)S(1)}, u32[]{:S(2)}, u32[]{:S(2)}) collective-permute-start(bf16[4,128,128]{2,1,0:T(8,128)(2,1)S(1)} %get-tuple-element.81), channel_id=1, source_target_pairs={{0,32},{32,64},{64,96},{96,0},{1,33},{33,65},{65,97},{97,1},{2,34}... | collective-permute-start | bytes 393224 | tf_op jit(solution)/shard_map/ppermute | solution.py:375
  96.7 3.8 %own_mine.1 = (f32[2,256,1152]{2,1,0:T(8,128)S(1)}, f32[1024,128]{1,0:T(8,128)S(1)}) custom-call(s32[3]{0:T(128)S(1)} %pad_add_fusion.refs_0_, s32[8]{0:T(128)S(1)} %copy-done.4, bf16[8,272,128]{2,1,0:T(8,128)(2,1)S(1)} %maximum_dynamic-update-slice_fusion.refs_2_, ...), custom_call_target="tpu_custom_call", output_to_operand_aliasing={{0}: (4, {}), {1}: (5, {})} | custom-call | flops 134217728 | bytes 262144 | tf_op jit(solution)/shard_map/own_mine/pallas_call | solution.py:242
  100.5 8.0 %collective-permute-done.13.chip = bf16[256,1152]{1,0:T(8,128)(2,1)S(1)} collective-permute-done((bf16[256,1152]{1,0:T(8,128)(2,1)S(1)}, bf16[256,1152]{1,0:T(8,128)(2,1)S(1)}, u32[]{:S(2)}, u32[]{:S(2)}) %collective-permute-start.13) | collective-permute-done | bytes 589856 | tf_op jit(solution)/shard_map/ppermute | solution.py:372
  108.5 1.3 %close.1 = (f32[1024,128]{1,0:T(8,128)}, f32[1024,128]{1,0:T(8,128)}, f32[128,128]{1,0:T(8,128)}, f32[128,128]{1,0:T(8,128)}) custom-call(f32[2,256,1152]{2,1,0:T(8,128)S(1)} %get-tuple-element.84.own, f32[256,1152]{1,0:T(8,128)S(1)} %collective-permute-done.12.core, bf16[256,1152]{1,0:T(8,128)(2,1)S(1)} %collective-permute-done.13.chip), custom_call_target="tpu_custom_call" | custom-call | tf_op jit(solution)/shard_map/close/pallas_call | solution.py:299
  113.1 9.8 %all_to_all.10 = bf16[8,128,128]{2,1,0:T(8,128)(2,1)S(1)} all-to-all(bf16[8,128,128]{2,1,0:T(8,128)(2,1)S(1)} %finish.1), channel_id=1, replica_groups=mesh['y'=4,'xh'=2,'c'=2,'z'=4,'xl'=2] {'z','xl'}, dimensions={0} | all-to-all | bytes 524288 | tf_op jit(solution)/shard_map/all_to_all | solution.py:384
  (51 shorter events, 6.5 us)
Async XLA Ops:
  0.6 11.0 %copy-start.5 = (f32[128,8]{0,1:T(8,128)S(1)}, f32[128,8]{0,1:T(8,128)}, u32[]{:S(2)}) copy-start(f32[128,8]{0,1:T(8,128)} %param.14) | copy-start | bytes 12292
  0.6 36.0 %copy-start.4 = (s32[8]{0:T(128)S(1)}, s32[8]{0:T(128)}, u32[]{:S(2)}) copy-start(s32[8]{0:T(128)} %refs_1_.17) | copy-start | bytes 100
  3.1 17.8 %collective-permute-start.5 = (bf16[2304,128]{1,0:T(8,128)(2,1)S(1)}, bf16[2304,128]{1,0:T(8,128)(2,1)S(1)}, u32[]{:S(2)}, u32[]{:S(2)}) collective-permute-start(bf16[2304,128]{1,0:T(8,128)(2,1)S(1)} %get-tuple-element.55.refs_4_.refs_3_), channel_id=1, source_target_pairs={{0,16},{16,0},{1,17},{17,1},{2,18},{18,2},{3,19},{19,3},{4,20},{20... | collective-permute-start | bytes 1769480 | tf_op jit(solution)/shard_map/ppermute | solution.py:341
  6.3 23.1 %all-to-all-start = ((bf16[8,272,128]{2,1,0:T(8,128)(2,1)}), bf16[8,272,128]{2,1,0:T(8,128)(2,1)S(1)}, u32[]{:S(2)}, u32[]{:S(2)}) async-start(bf16[8,272,128]{2,1,0:T(8,128)(2,1)} %get-tuple-element.54), calls=%async_computation | async-start | bytes 1114112 | tf_op jit(solution)/shard_map/all_to_all | solution.py:343
  11.6 30.9 %collective-permute-start.4 = (bf16[2304,128]{1,0:T(8,128)(2,1)S(1)}, bf16[2304,128]{1,0:T(8,128)(2,1)S(1)}, u32[]{:S(2)}, u32[]{:S(2)}) collective-permute-start(bf16[2304,128]{1,0:T(8,128)(2,1)S(1)} %get-tuple-element.55.refs_4_.refs_3_), channel_id=1, source_target_pairs={{0,8},{8,0},{1,9},{9,1},{2,10},{10,2},{3,11},{11,3},{4,12},{12,4},... | collective-permute-start | bytes 1769480 | tf_op jit(solution)/shard_map/ppermute | solution.py:342
  20.9 15.6 %collective-permute-start.6 = (bf16[2304,128]{1,0:T(8,128)(2,1)S(1)}, bf16[2304,128]{1,0:T(8,128)(2,1)S(1)}, u32[]{:S(2)}, u32[]{:S(2)}) collective-permute-start(bf16[2304,128]{1,0:T(8,128)(2,1)S(1)} %collective-permute-done.5.refs_3_.refs_4_), channel_id=1, source_target_pairs={{0,8},{8,0},{1,9},{9,1},{2,10},{10,2},{3,11},{11,3},{4,12},{12,4},... | collective-permute-start | bytes 1769480 | tf_op jit(solution)/shard_map/ppermute | solution.py:344
  30.3 15.5 %collective-permute-start.2 = (bf16[4,272,128]{2,1,0:T(8,128)(2,1)}, bf16[4,272,128]{2,1,0:T(8,128)(2,1)}, u32[]{:S(2)}, u32[]{:S(2)}) collective-permute-start(bf16[4,272,128]{2,1,0:T(8,128)(2,1)} %get-tuple-element.91), channel_id=1, source_target_pairs={{0,96},{32,0},{64,32},{96,64},{1,97},{33,1},{65,33},{97,65},{2,98}... | collective-permute-start | bytes 835592 | tf_op jit(solution)/shard_map/ppermute | solution.py:347
  33.3 12.5 %collective-permute-start.3 = (bf16[4,272,128]{2,1,0:T(8,128)(2,1)}, bf16[4,272,128]{2,1,0:T(8,128)(2,1)}, u32[]{:S(2)}, u32[]{:S(2)}) collective-permute-start(bf16[4,272,128]{2,1,0:T(8,128)(2,1)} %get-tuple-element.92), channel_id=1, source_target_pairs={{0,32},{32,64},{64,96},{96,0},{1,33},{33,65},{65,97},{97,1},{2,34}... | collective-permute-start | bytes 835592 | tf_op jit(solution)/shard_map/ppermute | solution.py:348
  33.3 23.0 %collective-permute-start = (bf16[4,272,128]{2,1,0:T(8,128)(2,1)}, bf16[4,272,128]{2,1,0:T(8,128)(2,1)S(1)}, u32[]{:S(2)}, u32[]{:S(2)}) collective-permute-start(bf16[4,272,128]{2,1,0:T(8,128)(2,1)} %get-tuple-element.92), channel_id=1, source_target_pairs={{0,96},{32,0},{64,32},{96,64},{1,97},{33,1},{65,33},{97,65},{2,98}... | collective-permute-start | bytes 835592 | tf_op jit(solution)/shard_map/ppermute | solution.py:349
  36.5 19.7 %collective-permute-start.1 = (bf16[4,272,128]{2,1,0:T(8,128)(2,1)}, bf16[4,272,128]{2,1,0:T(8,128)(2,1)S(1)}, u32[]{:S(2)}, u32[]{:S(2)}) collective-permute-start(bf16[4,272,128]{2,1,0:T(8,128)(2,1)} %get-tuple-element.91), channel_id=1, source_target_pairs={{0,32},{32,64},{64,96},{96,0},{1,33},{33,65},{65,97},{97,1},{2,34}... | collective-permute-start | bytes 835592 | tf_op jit(solution)/shard_map/ppermute | solution.py:350
  45.8 23.5 %collective-permute-start.7 = (bf16[4,272,128]{2,1,0:T(8,128)(2,1)}, bf16[4,272,128]{2,1,0:T(8,128)(2,1)S(1)}, u32[]{:S(2)}, u32[]{:S(2)}) collective-permute-start(bf16[4,272,128]{2,1,0:T(8,128)(2,1)} %collective-permute-done.2.refs_2_), channel_id=1, source_target_pairs={{0,96},{32,0},{64,32},{96,64},{1,97},{33,1},{65,33},{97,65},{2,98}... | collective-permute-start | bytes 835592 | tf_op jit(solution)/shard_map/ppermute | solution.py:357
  49.1 20.2 %collective-permute-start.8 = (bf16[4,272,128]{2,1,0:T(8,128)(2,1)}, bf16[4,272,128]{2,1,0:T(8,128)(2,1)S(1)}, u32[]{:S(2)}, u32[]{:S(2)}) collective-permute-start(bf16[4,272,128]{2,1,0:T(8,128)(2,1)} %collective-permute-done.3.refs_3_), channel_id=1, source_target_pairs={{0,32},{32,64},{64,96},{96,0},{1,33},{33,65},{65,97},{97,1},{2,34}... | collective-permute-start | bytes 835592 | tf_op jit(solution)/shard_map/ppermute | solution.py:358
  75.3 9.6 %collective-permute-start.9 = (f32[256,1152]{1,0:T(8,128)S(1)}, f32[256,1152]{1,0:T(8,128)S(1)}, u32[]{:S(2)}, u32[]{:S(2)}) collective-permute-start(f32[256,1152]{1,0:T(8,128)S(1)} %slice_bitcast_fusion.1), channel_id=1, source_target_pairs={{0,8},{8,0},{1,9},{9,1},{2,10},{10,2},{3,11},{11,3},{4,12},{12,4},... | collective-permute-start | bytes 3538952 | tf_op jit(solution)/shard_map/ppermute | solution.py:368
  75.7 9.4 %collective-permute-start.10 = (bf16[4,128,128]{2,1,0:T(8,128)(2,1)S(1)}, bf16[4,128,128]{2,1,0:T(8,128)(2,1)S(1)}, u32[]{:S(2)}, u32[]{:S(2)}) collective-permute-start(bf16[4,128,128]{2,1,0:T(8,128)(2,1)S(1)} %get-tuple-element.68), channel_id=1, source_target_pairs={{0,32},{32,64},{64,96},{96,0},{1,33},{33,65},{65,97},{97,1},{2,34}... | collective-permute-start | bytes 393224 | tf_op jit(solution)/shard_map/ppermute | solution.py:364
  75.7 9.3 %collective-permute-start.11 = (bf16[4,128,128]{2,1,0:T(8,128)(2,1)S(1)}, bf16[4,128,128]{2,1,0:T(8,128)(2,1)S(1)}, u32[]{:S(2)}, u32[]{:S(2)}) collective-permute-start(bf16[4,128,128]{2,1,0:T(8,128)(2,1)S(1)} %get-tuple-element.78), channel_id=1, source_target_pairs={{0,96},{32,0},{64,32},{96,64},{1,97},{33,1},{65,33},{97,65},{2,98}... | collective-permute-start | bytes 393224 | tf_op jit(solution)/shard_map/ppermute | solution.py:365
  91.2 17.3 %collective-permute-start.12 = (f32[256,1152]{1,0:T(8,128)S(1)}, f32[256,1152]{1,0:T(8,128)S(1)}, u32[]{:S(2)}, u32[]{:S(2)}) collective-permute-start(f32[256,1152]{1,0:T(8,128)S(1)} %slice_bitcast_fusion), channel_id=1, source_target_pairs={{0,8},{8,0},{1,9},{9,1},{2,10},{10,2},{3,11},{11,3},{4,12},{12,4},... | collective-permute-start | bytes 3538952 | tf_op jit(solution)/shard_map/ppermute | solution.py:377
  91.3 17.2 %collective-permute-start.13 = (bf16[256,1152]{1,0:T(8,128)(2,1)S(1)}, bf16[256,1152]{1,0:T(8,128)(2,1)S(1)}, u32[]{:S(2)}, u32[]{:S(2)}) collective-permute-start(bf16[256,1152]{1,0:T(8,128)(2,1)S(1)} %fusion), channel_id=1, source_target_pairs={{0,16},{16,0},{1,17},{17,1},{2,18},{18,2},{3,19},{19,3},{4,20},{20... | collective-permute-start | bytes 1769480 | tf_op jit(solution)/shard_map/ppermute | solution.py:372
  93.2 16.7 %collective-permute-start.16 = (bf16[8,128,128]{2,1,0:T(8,128)(2,1)S(1)}, bf16[8,128,128]{2,1,0:T(8,128)(2,1)S(1)}, u32[]{:S(2)}, u32[]{:S(2)}) collective-permute-start(bf16[8,128,128]{2,1,0:T(8,128)(2,1)S(1)} %get-tuple-element.76), channel_id=1, source_target_pairs={{0,64},{32,96},{64,0},{96,32},{1,65},{33,97},{65,1},{97,33},{2,66}... | collective-permute-start | bytes 786440 | tf_op jit(solution)/shard_map/ppermute | solution.py:370
  94.7 15.2 %collective-permute-start.14 = (bf16[4,128,128]{2,1,0:T(8,128)(2,1)S(1)}, bf16[4,128,128]{2,1,0:T(8,128)(2,1)S(1)}, u32[]{:S(2)}, u32[]{:S(2)}) collective-permute-start(bf16[4,128,128]{2,1,0:T(8,128)(2,1)S(1)} %get-tuple-element.87), channel_id=1, source_target_pairs={{0,96},{32,0},{64,32},{96,64},{1,97},{33,1},{65,33},{97,65},{2,98}... | collective-permute-start | bytes 393224 | tf_op jit(solution)/shard_map/ppermute | solution.py:376
  95.1 15.4 %collective-permute-start.15 = (bf16[4,128,128]{2,1,0:T(8,128)(2,1)S(1)}, bf16[4,128,128]{2,1,0:T(8,128)(2,1)S(1)}, u32[]{:S(2)}, u32[]{:S(2)}) collective-permute-start(bf16[4,128,128]{2,1,0:T(8,128)(2,1)S(1)} %get-tuple-element.81), channel_id=1, source_target_pairs={{0,32},{32,64},{64,96},{96,0},{1,33},{33,65},{65,97},{97,1},{2,34}... | collective-permute-start | bytes 393224 | tf_op jit(solution)/shard_map/ppermute | solution.py:375
  109.8 0.7 copy-start
  110.5 0.6 copy-start.2
  111.2 0.9 copy-start.1
  112.1 0.9 copy-start.3

commit v3 on v2

v3 whole, which is shorter than its diff:
```python
import functools

import jax
import jax.numpy as jnp
from jax import lax
from jax.experimental import pallas as pl
from jax.experimental.pallas import tpu as pltpu
from jax.sharding import Mesh
from jax.sharding import PartitionSpec as P

F32 = jnp.float32
BF16 = jnp.bfloat16
HD = 128
GROUP = 8
BLOCK = 128
NBLK = 16
PK = 1024
RK = 128
KW = PK + RK
QR = BLOCK * GROUP
SRC = 8
SUB = BLOCK // SRC
DROW = 2 * BLOCK
LROW = DROW + 8
PAY = LROW + 8
SCALE = HD ** (-0.5)
LOG2E = 1.4426950408889634
C2 = SCALE * LOG2E

NN = (((1,), (0,)), ((), ()))
NT = (((1,), (1,)), ((), ()))

Y, XH, C, Z, XL = "y", "xh", "c", "z", "xl"
BULK = (Z, XL)


def dot(a, b, dims):
    return lax.dot_general(a, b, dims, preferred_element_type=F32)


def held(*arrays):
    return [pltpu.with_memory_space_constraint(a, pltpu.VMEM) for a in arrays]


ANYSPEC = pl.BlockSpec(memory_space=pl.ANY)
VSPEC = pl.BlockSpec(memory_space=pltpu.VMEM)
SSPEC = pl.BlockSpec(memory_space=pltpu.SMEM)


def pieces_of(x):
    a = x.astype(BF16).astype(F32)
    b = (x - a).astype(BF16).astype(F32)
    return a, b, x - a - b


def pack_kernel(q_in, g_in, o_in, pay, q, g, o, sems):
    loads = [
        pltpu.make_async_copy(src, dst, sems.at[n])
        for n, (src, dst) in enumerate(((q_in, q), (g_in, g), (o_in, o)))
    ]
    for copy in loads:
        copy.start()
    for copy in loads:
        copy.wait()
    ones = jnp.ones((16, HD), BF16)
    row = lax.broadcasted_iota(jnp.int32, (16, BLOCK), 0)
    for b in range(SRC):
        prods = []
        for h in range(GROUP):
            cols = slice((b * GROUP + h) * HD, (b * GROUP + h + 1) * HD)
            qh, gh = q[:, cols], g[:, cols]
            pay[b, h * SUB : (h + 1) * SUB, :] = qh
            pay[b, BLOCK + h * SUB : BLOCK + (h + 1) * SUB, :] = gh
            prods.append(gh.astype(F32) * o[:, cols].astype(F32))
        prod = jnp.concatenate(prods, axis=0)
        high = prod.astype(BF16)
        low = (prod - high.astype(F32)).astype(BF16)
        d1, d2, d3 = pieces_of(dot(ones, high, NT) + dot(ones, low, NT))
        rows = jnp.where(row == 0, d1, jnp.where(row == 1, d2, jnp.where(row == 2, d3, 0.0)))
        pay[b, DROW:PAY, :] = rows.astype(BF16)


def in_hbm(arrays):
    return [pltpu.with_memory_space_constraint(a, pltpu.HBM) for a in arrays]


def pack(*arrays):
    return pl.pallas_call(
        pack_kernel,
        in_specs=[ANYSPEC] * 3,
        out_specs=VSPEC,
        out_shape=pltpu.VMEM((SRC, PAY, HD), BF16),
        scratch_shapes=[pltpu.VMEM((SUB, SRC * GROUP * HD), BF16)] * 3
        + [pltpu.SemaphoreType.DMA((3,))],
        compiler_params=pltpu.CompilerParams(vmem_limit_bytes=8 << 20),
        name="pack",
    )(*in_hbm(arrays))


def join_kernel(pk, rk, pv, rv, kv, sems):
    copies, at = [], 0
    for n, (src, rows) in enumerate(((pk, PK), (rk, RK), (pv, PK), (rv, RK))):
        copies.append(pltpu.make_async_copy(src, kv.at[pl.ds(at, rows)], sems.at[n]))
        at += rows
    for copy in copies:
        copy.start()
    for copy in copies:
        copy.wait()


def join(*arrays):
    return pl.pallas_call(
        join_kernel,
        in_specs=[ANYSPEC] * 4,
        out_specs=VSPEC,
        out_shape=pltpu.VMEM((2 * KW, HD), BF16),
        scratch_shapes=[pltpu.SemaphoreType.DMA((4,))],
        name="join",
    )(*in_hbm(arrays))


def column(rows):
    line = jnp.concatenate([rows[s : s + 1, :] for s in range(SRC)], axis=1)
    return jnp.broadcast_to(line, (HD, QR)).T


def pick(n, values):
    out = values[0]
    for m in range(1, len(values)):
        out = jnp.where(n == m, values[m], out)
    return out


def tiles_kernel(cfg, *refs):
    units, far, have, final = cfg
    nu = len(units)
    refs = list(refs)

    def take(n):
        out = refs[:n]
        del refs[:n]
        return out

    place, lengths = take(2)
    pays = [r for n in units for r in take(2 if n == 2 else 1)]
    key_in = take(2)
    take(have["dq"] + have["sums"] + have["out"])
    dqs, sums = take(2)
    out = take(1)[0] if final else None
    qs, gs, qt, gt, keys, scalars, log_col, delta_col = refs
    y, xh, c = place[0], place[1], place[2]

    def step(t, carry):
        u, j = t // 2, t % 2
        back = pick(u, units)
        at_pay = 0
        for n in range(nu):
            parts = pays[at_pay : at_pay + (2 if units[n] == 2 else 1)]
            at_pay += len(parts)

            @pl.when(t == 2 * n)
            def _():
                rows, srcs = QR // len(parts), SRC // len(parts)
                for m, pay in enumerate(parts):
                    span = slice(m * rows, (m + 1) * rows)
                    qs[span, :] = pay[:, 0:BLOCK, :].reshape(rows, HD)
                    gs[span, :] = pay[:, BLOCK : 2 * BLOCK, :].reshape(rows, HD)
                    scalars[m * srcs : (m + 1) * srcs] = pay[:, DROW:PAY, :].astype(F32)

        @pl.when(j == 0)
        def _():
            add = lambda n: scalars[:, n, :] + scalars[:, n + 1, :] + scalars[:, n + 2, :]
            delta_col[...] = column(add(0))
            log_col[...] = column(add(LROW - DROW))
            qt[...] = qs[...].T
            gt[...] = gs[...].T
            if not have["started"]:
                dqs[back] = jnp.zeros((QR, HD), F32)

        for n in range(2):

            @pl.when(j == n)
            def _():
                keys[...] = key_in[n][...]

        def products(at, width):
            s = dot(qs[...], keys[at : at + width, :], NT)
            dp = dot(gs[...], keys[KW + at : KW + at + width, :], NT)
            return s, dp

        def grads(at, width, s, dp, allowed):
            wide = lambda col: jnp.concatenate([col[...]] * (width // HD), axis=1)
            p = jnp.exp2(s * C2 - wide(log_col))
            if allowed is not None:
                p = jnp.where(allowed, p, 0.0)
            ds = (p * (dp - wide(delta_col))).astype(BF16)
            p = p.astype(BF16)
            dk = dot(qt[...], ds, NN)
            dv = dot(gt[...], p, NN)
            cols = slice(at, at + width)
            if have["sums"] or at >= PK:
                sums[j, 0:HD, cols] += dk
                sums[j, HD : 2 * HD, cols] += dv
            else:
                sums[j, 0:HD, cols] = dk
                sums[j, HD : 2 * HD, cols] = dv
            return dot(ds, keys[at : at + width, :], NN)

        if not have["sums"]:
            sums[j, :, PK:KW] = jnp.zeros((2 * HD, RK), F32)
        part = 256
        total = None
        ahead = products(0, part)
        for n in range(PK // part):
            s, dp = ahead
            if n + 1 < PK // part:
                ahead = products((n + 1) * part, part)
            term = grads(n * part, part, s, dp, None)
            total = term if total is None else total + term
        dqs[back] += total

        qi = 4 * ((y + back) % 4) + 2 * xh + c
        kj = 4 * y + 2 * ((1 - xh) if far else xh) + (c + j - 2 * c * j)
        seen, end = kj <= qi, 0
        for r in range(lengths.shape[0]):
            end = end + lengths[r]
            seen = seen & ((end <= kj) | (end > qi))

        @pl.when(seen)
        def _():
            row = lax.broadcasted_iota(jnp.int32, (QR, RK), 0)
            key_at = lax.broadcasted_iota(jnp.int32, (QR, RK), 1)
            token = (row // BLOCK) * SUB + row % SUB
            allowed = (kj < qi) | (key_at <= token)
            s, dp = products(PK, RK)
            dqs[back] += grads(PK, RK, s, dp, allowed)

        if final:

            @pl.when(j == 1)
            def _():
                done = (dqs[back] * SCALE).astype(BF16)
                out[(y + back) % 4] = done.reshape(SRC, BLOCK, HD)

        return carry

    lax.fori_loop(0, 2 * nu, step, 0)


def tiles(name, units, far, place, lengths, pays, keys, dqs, sums, out=None, started=False, final=False):
    have = {"dq": dqs is not None, "sums": sums is not None, "out": out is not None, "started": started}
    operands = held(*pays, *keys)
    aliases = {}
    for n, state in enumerate((dqs, sums, out)):
        if state is not None:
            aliases[2 + len(operands)] = n
            operands += held(state)
    shapes = [pltpu.VMEM((4, QR, HD), F32), pltpu.VMEM((2, 2 * HD, KW), F32)]
    if final:
        shapes.append(pltpu.VMEM((4, SRC, BLOCK, HD), BF16))
    return pl.pallas_call(
        functools.partial(tiles_kernel, (tuple(units), far, have, final)),
        in_specs=[SSPEC] * 2 + [VSPEC] * len(operands),
        out_specs=[VSPEC] * len(shapes),
        out_shape=shapes,
        scratch_shapes=[
            pltpu.VMEM((QR, HD), BF16),
            pltpu.VMEM((QR, HD), BF16),
            pltpu.VMEM((HD, QR), BF16),
            pltpu.VMEM((HD, QR), BF16),
            pltpu.VMEM((2 * KW, HD), BF16),
            pltpu.VMEM((SRC, PAY - DROW, HD), F32),
            pltpu.VMEM((QR, HD), F32),
            pltpu.VMEM((QR, HD), F32),
        ],
        input_output_aliases=aliases,
        compiler_params=pltpu.CompilerParams(vmem_limit_bytes=24 << 20),
        cost_estimate=pl.CostEstimate(
            flops=1, bytes_accessed=1, transcendentals=0
        ),
        name=name,
    )(place, lengths, *operands)


def finish_kernel(parts, out):
    for b in range(SRC):
        for h in range(GROUP):
            rows = slice(h * SUB, (h + 1) * SUB)
            terms = [parts[n * SRC + b, rows, :].astype(F32) for n in range(4)]
            col = (b * GROUP + h) * HD
            out[:, col : col + HD] = (terms[0] + terms[1] + terms[2] + terms[3]).astype(BF16)


def finish(parts):
    return pl.pallas_call(
        finish_kernel,
        in_specs=[VSPEC],
        out_specs=VSPEC,
        out_shape=jax.ShapeDtypeStruct((SUB, SRC * GROUP * HD), BF16),
        name="finish",
    )(*held(parts))


def close_kernel(own, core, chip, dk, dv, drk, drv):
    def total(rows, cols):
        part = own[0, rows, cols] + core[rows, cols] + chip[rows, cols].astype(F32)
        return part.T

    keys, values = slice(0, HD), slice(HD, 2 * HD)
    dk[...] = total(keys, slice(0, PK)) * SCALE
    drk[...] = total(keys, slice(PK, KW)) * SCALE
    dv[...] = total(values, slice(0, PK))
    drv[...] = total(values, slice(PK, KW))


def close(own, core, chip):
    shape = lambda rows: jax.ShapeDtypeStruct((rows, HD), F32)
    return pl.pallas_call(
        close_kernel,
        in_specs=[VSPEC] * 3,
        out_specs=[VSPEC] * 4,
        out_shape=[shape(PK), shape(PK), shape(RK), shape(RK)],
        compiler_params=pltpu.CompilerParams(vmem_limit_bytes=16 << 20),
        name="close",
    )(*held(own, core, chip))


def shift(n, s):
    return [(i, (i + s) % n) for i in range(n)]


def after(values, *earlier):
    return lax.optimization_barrier((values, earlier))[0]


def shards(
    queries,
    out_grad,
    attn_out,
    log_totals,
    prompt_keys,
    prompt_values,
    rollout_keys,
    rollout_values,
    rollout_blocks,
):
    place = jnp.stack([lax.axis_index(Y), lax.axis_index(XH), lax.axis_index(C)])
    place = place.astype(jnp.int32)
    to_next, to_last, swap = shift(4, 1), shift(4, -1), shift(2, 1)

    logs = (log_totals * LOG2E).reshape(SRC, SUB, GROUP).transpose(0, 2, 1).reshape(SRC, 1, BLOCK)
    l1 = lax.reduce_precision(logs, 8, 7)
    l2 = lax.reduce_precision(logs - l1, 8, 7)
    logs = [p.astype(BF16) for p in (l1, l2, logs - l1 - l2)]
    logs = jnp.concatenate(logs + [jnp.zeros((SRC, PAY - LROW - 3, BLOCK), BF16)], axis=1)

    payload = pack(queries, out_grad, attn_out)
    own = lax.all_to_all(payload, BULK, split_axis=0, concat_axis=0, tiled=True)
    kv_own = join(*after((prompt_keys, rollout_keys, prompt_values, rollout_values), payload))
    kv_x = lax.ppermute(kv_own, XH, swap)
    kv_c = lax.ppermute(kv_own, C, swap)
    kv_xc = lax.ppermute(kv_x, C, swap)
    own = own.at[:, LROW:PAY, :].set(logs)
    up = lax.ppermute(own, Y, to_last)
    down = lax.ppermute(own, Y, to_next)

    def run(name, units, far, *rest, **kw):
        keys = [kv_x, kv_xc] if far else [kv_own, kv_c]
        return tiles(name, units, far, place, rollout_blocks, rest[0], keys, *rest[1:], **kw)

    dqs, g_here = run("own_here", [0], False, [own], None, None)
    dqs, g_far, out = run("own_far", [0], True, [own], dqs, None, started=True, final=True)
    up, down = after((up, down), out)
    opp = [lax.ppermute(up[: SRC // 2], Y, to_last), lax.ppermute(down[SRC // 2 :], Y, to_next)]
    dqs, g_far = run("near_far", [1, 3], True, [up, down], dqs, g_far)
    opp = after(opp, dqs)
    dqs, g_far = run("opp_far", [2], True, opp, dqs, g_far)
    from_core = lax.ppermute(g_far[1], C, swap)
    dqs, g_here, out = run("up_here", [1], False, [up], dqs, g_here, out, started=True, final=True)
    to_chip = (g_far[0] + after(from_core, dqs)).astype(BF16)
    from_chip = lax.ppermute(to_chip, XH, swap)
    dqs = after(dqs, to_chip)
    dqs, g_here, out = run(
        "rest_here", [3, 2], False, [down, *opp], dqs, g_here, out, started=True, final=True
    )
    from_c = lax.ppermute(g_here[1], C, swap)
    parts = lax.all_to_all(
        out.reshape(4 * SRC, BLOCK, HD), (Y,) + BULK, split_axis=0, concat_axis=0, tiled=True
    )
    dk, dv, drk, drv = close(g_here, from_c, from_chip)
    query_grad = finish(after(parts, dk))
    return (query_grad, dk, dv, drk, drv)


def solution(mesh):
    fine = Mesh(mesh.devices.reshape(4, 2, 2, 4, 2), (Y, XH, C, Z, XL))
    hold, bulk = (Y, XH, C), (Z, XL)
    tokens = P(hold + bulk, None)
    split = P(hold, bulk)
    return jax.shard_map(
        shards,
        mesh=fine,
        in_specs=(tokens, tokens, tokens, split, split, split, split, split, P()),
        out_specs=(tokens, split, split, split, split),
        check_vma=False,
    )
```

time: 124 us -> 131 us (1.056)
  waiting for transfers between devices: 25.5 us -> 42 us
  blocking collectives: 9.77 us -> 0 us
  Pallas kernels: 54.9 us -> 60.3 us
  starting transfers between devices: 27.2 us -> 22.4 us
  local copies, waits for them, and re-layouts: 5.07 us -> 3.41 us
  other arithmetic: 0.29 us -> 1.73 us
    ppermute x1, waiting for transfers between devices: 8.01 us -> 24.4 us  [shards(): from_chip = lax.ppermute(to_chip, XH, swap)]
    ppermute x11 -> x4, starting transfers between devices: 16.4 us -> 5.33 us  [the longest x1 1.87 us: shards(): lax.ppermute(up[:SRC // 2], Y, to_last)]
    all_to_all x1 -> x0, blocking collectives: 9.77 us -> none  [shards(): dq = lax.all_to_all(dq, BULK, split_axis=0, concat_axis=0, tiled=True)]
    all_to_all x0 -> x1, starting transfers between devices: none -> 4.89 us  [shards(): lax.all_to_all(out.reshape(4 * SRC, BLOCK, HD), (Y,) + BULK, split_axis=0...]
    pallas_call x11 -> x9, Pallas kernels: 53.5 us -> 57.7 us  [the longest x6 52.2 us: tiles(): pl.pallas_call(functools.partial(tiles_kernel, (tuple(units), far, have,...]
    unnamed x12 -> x8, local copies, waits for them, and re-layouts: 3.11 us -> 0.02 us
  transfers between devices with their start and end apart: 18 -> 12, of which waited for: 3 -> 3; matrix products, arithmetic and copies ran while one was open for 1% -> 1% of each run, Pallas kernels for 33% -> 28%
where the time goes in v3:
time: 131 us
  Pallas kernels  60.3 us (46%)
  waiting for transfers between devices  42 us (32%)
  starting transfers between devices  22.4 us (17%)
  local copies, waits for them, and re-layouts  3.41 us (3%)
  other arithmetic  1.73 us (1%)
    pallas_call x6, Pallas kernels, tiles(): pl.pallas_call(functools.partial(tiles_kernel, (tuple(units), far, have,...  52.2 us
    ppermute x1, waiting for transfers between devices, shards(): from_chip = lax.ppermute(to_chip, XH, swap)  24.4 us
    ppermute x1, waiting for transfers between devices, shards(): kv_x = lax.ppermute(kv_own, XH, swap)  9.09 us
    all_to_all x1, waiting for transfers between devices, shards(): own = lax.all_to_all(payload, BULK, split_axis=0, concat_axis=0, tiled=True)  8.44 us
    all_to_all x1, starting transfers between devices, shards(): own = lax.all_to_all(payload, BULK, split_axis=0, concat_axis=0, tiled=True)  5.34 us
    all_to_all x1, starting transfers between devices, shards(): lax.all_to_all(out.reshape(4 * SRC, BLOCK, HD), (Y,) + BULK, split_axis=0...  4.89 us
    ppermute x1, starting transfers between devices, shards(): kv_x = lax.ppermute(kv_own, XH, swap)  3.19 us
    ppermute x1, starting transfers between devices, shards(): from_chip = lax.ppermute(to_chip, XH, swap)  2.9 us
  transfers between devices with their start and end apart: 12, of which 3 were waited for; matrix products, arithmetic and copies ran while one was open for 1% of the time, Pallas kernels for 28%

profile of v3, /device:TPU:0, one launch (start us, length us, event | category | flops | bytes accessed | tf_op | source)
XLA Modules:
  0.0 130.7 jit_solution(13890495421419722957)
XLA Ops:
  0.7 2.3 %pack.1 = bf16[8,272,128]{2,1,0:T(8,128)(2,1)} custom-call(bf16[16,8192]{1,0:T(8,128)(2,1)} %q_in.1, bf16[16,8192]{1,0:T(8,128)(2,1)} %g_in.1, bf16[16,8192]{1,0:T(8,128)(2,1)} %o_in.1), custom_call_target="tpu_custom_call" | custom-call | tf_op jit(solution)/shard_map/pack/pallas_call | solution.py:88
  3.0 1.1 join.1.refs_3_.refs_5_
  4.1 3.2 %collective-permute-start.2 = (bf16[2304,128]{1,0:T(8,128)(2,1)S(1)}, bf16[2304,128]{1,0:T(8,128)(2,1)}, u32[]{:S(2)}, u32[]{:S(2)}) collective-permute-start(bf16[2304,128]{1,0:T(8,128)(2,1)S(1)} %join.1.refs_3_.refs_5_), channel_id=1, source_target_pairs={{0,16},{16,0},{1,17},{17,1},{2,18},{18,2},{3,19},{19,3},{4,20},{20... | collective-permute-start | bytes 1769480 | tf_op jit(solution)/shard_map/ppermute | solution.py:360
  7.3 5.3 %all-to-all-start = ((bf16[8,272,128]{2,1,0:T(8,128)(2,1)}), bf16[8,272,128]{2,1,0:T(8,128)(2,1)}, u32[]{:S(2)}, u32[]{:S(2)}) async-start(bf16[8,272,128]{2,1,0:T(8,128)(2,1)} %pack.1), calls=%async_computation | async-start | bytes 1114112 | tf_op jit(solution)/shard_map/all_to_all | solution.py:358
  12.9 9.1 %collective-permute-done.2.refs_3_.refs_4_ = bf16[2304,128]{1,0:T(8,128)(2,1)} collective-permute-done((bf16[2304,128]{1,0:T(8,128)(2,1)S(1)}, bf16[2304,128]{1,0:T(8,128)(2,1)}, u32[]{:S(2)}, u32[]{:S(2)}) %collective-permute-start.2) | collective-permute-done | bytes 589856 | tf_op jit(solution)/shard_map/ppermute | solution.py:360
  22.0 8.4 %all-to-all-done = bf16[8,272,128]{2,1,0:T(8,128)(2,1)} async-done(((bf16[8,272,128]{2,1,0:T(8,128)(2,1)}), bf16[8,272,128]{2,1,0:T(8,128)(2,1)}, u32[]{:S(2)}, u32[]{:S(2)}) %all-to-all-start) | async-done | bytes 557088 | tf_op jit(solution)/shard_map/all_to_all | solution.py:358
  31.2 1.6 %collective-permute-start.1 = (bf16[8,272,128]{2,1,0:T(8,128)(2,1)}, bf16[8,272,128]{2,1,0:T(8,128)(2,1)}, u32[]{:S(2)}, u32[]{:S(2)}) collective-permute-start(bf16[8,272,128]{2,1,0:T(8,128)(2,1)} %maximum_dynamic-update-slice_fusion.refs_2_), channel_id=1, source_target_pairs={{0,32},{32,64},{64,96},{96,0},{1,33},{33,65},{65,97},{97,1},{2,34}... | collective-permute-start | bytes 1671176 | tf_op jit(solution)/shard_map/ppermute | solution.py:365
  32.7 1.7 %collective-permute-start = (bf16[8,272,128]{2,1,0:T(8,128)(2,1)}, bf16[8,272,128]{2,1,0:T(8,128)(2,1)}, u32[]{:S(2)}, u32[]{:S(2)}) collective-permute-start(bf16[8,272,128]{2,1,0:T(8,128)(2,1)} %maximum_dynamic-update-slice_fusion.refs_2_), channel_id=1, source_target_pairs={{0,96},{32,0},{64,32},{96,64},{1,97},{33,1},{65,33},{97,65},{2,98}... | collective-permute-start | bytes 1671176 | tf_op jit(solution)/shard_map/ppermute | solution.py:364
  34.5 7.2 %own_here.1 = (f32[4,1024,128]{2,1,0:T(8,128)S(1)}, f32[2,256,1152]{2,1,0:T(8,128)S(1)}) custom-call(s32[3]{0:T(128)S(1)} %pad_add_fusion.refs_0_, s32[8]{0:T(128)S(1)} %copy-done.1, bf16[8,272,128]{2,1,0:T(8,128)(2,1)} %maximum_dynamic-update-slice_fusion.refs_2_, bf16[2304,128]{1,0:T(8,128)(2,1)S(1)} %join.1.refs_3_.refs_5_, ...), custom_call_target="tpu_custom_call" | custom-call | flops 1 | bytes 1 | tf_op jit(solution)/shard_map/own_here/pallas_call | solution.py:261
  41.7 6.8 %own_far.1 = (f32[4,1024,128]{2,1,0:T(8,128)S(1)}, f32[2,256,1152]{2,1,0:T(8,128)S(1)}, bf16[4,8,128,128]{3,2,1,0:T(8,128)(2,1)S(1)}) custom-call(s32[3]{0:T(128)S(1)} %pad_add_fusion.refs_0_, s32[8]{0:T(128)S(1)} %copy-done.1, bf16[8,272,128]{2,1,0:T(8,128)(2,1)} %maximum_dynamic-update-slice_fusion.refs_2_, ...), custom_call_target="tpu_custom_call", output_to_operand_aliasing={{0}: (5, {})} | custom-call | flops 1 | bytes 1 | tf_op jit(solution)/shard_map/own_far/pallas_call | solution.py:261
  48.6 1.0 slice.38
  49.6 1.0 slice.37
  50.5 1.9 %collective-permute-start.5 = (bf16[4,272,128]{2,1,0:T(8,128)(2,1)S(1)}, bf16[4,272,128]{2,1,0:T(8,128)(2,1)S(1)}, u32[]{:S(2)}, u32[]{:S(2)}) collective-permute-start(bf16[4,272,128]{2,1,0:T(8,128)(2,1)S(1)} %slice.37), channel_id=1, source_target_pairs={{0,96},{32,0},{64,32},{96,64},{1,97},{33,1},{65,33},{97,65},{2,98}... | collective-permute-start | bytes 835592 | tf_op jit(solution)/shard_map/ppermute | solution.py:374
  52.6 13.1 %near_far.1 = (f32[4,1024,128]{2,1,0:T(8,128)S(1)}, f32[2,256,1152]{2,1,0:T(8,128)S(1)}) custom-call(s32[3]{0:T(128)S(1)} %pad_add_fusion.refs_0_, s32[8]{0:T(128)S(1)} %copy-done.1, bf16[8,272,128]{2,1,0:T(8,128)(2,1)} %collective-permute-done.refs_2_, ...), custom_call_target="tpu_custom_call", output_to_operand_aliasing={{0}: (6, {}), {1}: (7, {})} | custom-call | flops 1 | bytes 1 | tf_op jit(solution)/shard_map/near_far/pallas_call | solution.py:261
  65.8 6.6 %opp_far.1 = (f32[4,1024,128]{2,1,0:T(8,128)S(1)}, f32[2,256,1152]{2,1,0:T(8,128)S(1)}) custom-call(s32[3]{0:T(128)S(1)} %pad_add_fusion.refs_0_, s32[8]{0:T(128)S(1)} %copy-done.1, bf16[4,272,128]{2,1,0:T(8,128)(2,1)S(1)} %collective-permute-done.5.refs_2_.refs_3_, ...), custom_call_target="tpu_custom_call", output_to_operand_aliasing={{0}: (6, {}), {1}: (7, {})} | custom-call | flops 1 | bytes 1 | tf_op jit(solution)/shard_map/opp_far/pallas_call | solution.py:261
  72.8 6.5 %up_here.1 = (f32[4,1024,128]{2,1,0:T(8,128)S(1)}, f32[2,256,1152]{2,1,0:T(8,128)S(1)}, bf16[4,8,128,128]{3,2,1,0:T(8,128)(2,1)S(1)}) custom-call(s32[3]{0:T(128)S(1)} %pad_add_fusion.refs_0_, s32[8]{0:T(128)S(1)} %copy-done.1, bf16[8,272,128]{2,1,0:T(8,128)(2,1)} %collective-permute-done.refs_2_, ...), custom_call_target="tpu_custom_call", output_to_operand_aliasing={{0}: (5, {}), {1}: (6, {}), {2}: (7, {})} | custom-call | flops 1 | bytes 1 | tf_op jit(solution)/shard_map/up_here/pallas_call | solution.py:261
  79.3 0.9 fusion
  80.3 11.9 %rest_here.1 = (f32[4,1024,128]{2,1,0:T(8,128)S(1)}, f32[2,256,1152]{2,1,0:T(8,128)S(1)}, bf16[4,8,128,128]{3,2,1,0:T(8,128)(2,1)S(1)}) custom-call(s32[3]{0:T(128)S(1)} %pad_add_fusion.refs_0_, s32[8]{0:T(128)S(1)} %copy-done.1, ...), custom_call_target="tpu_custom_call", output_to_operand_aliasing={{0}: (7, {}), {1}: (8, {}), {2}: (9, {})} | custom-call | flops 1 | bytes 1 | tf_op jit(solution)/shard_map/rest_here/pallas_call | solution.py:261
  92.2 1.1 slice_bitcast_fusion
  93.8 4.9 %all-to-all-start.1 = ((bf16[32,128,128]{2,1,0:T(8,128)(2,1)}), bf16[32,128,128]{2,1,0:T(8,128)(2,1)}, u32[]{:S(2)}, u32[]{:S(2)}) async-start(bf16[32,128,128]{2,1,0:T(8,128)(2,1)} %bitcast.17), calls=%async_computation.1 | async-start | bytes 2097152 | tf_op jit(solution)/shard_map/all_to_all | solution.py:387
  98.7 2.9 %collective-permute-start.9 = (bf16[256,1152]{1,0:T(8,128)(2,1)S(1)}, bf16[256,1152]{1,0:T(8,128)(2,1)S(1)}, u32[]{:S(2)}, u32[]{:S(2)}) collective-permute-start(bf16[256,1152]{1,0:T(8,128)(2,1)S(1)} %copy-done.2), channel_id=1, source_target_pairs={{0,16},{16,0},{1,17},{17,1},{2,18},{18,2},{3,19},{19,3},{4,20},{20... | collective-permute-start | bytes 1769480 | tf_op jit(solution)/shard_map/ppermute | solution.py:381
  101.6 24.4 %collective-permute-done.9.chip = bf16[256,1152]{1,0:T(8,128)(2,1)S(1)} collective-permute-done((bf16[256,1152]{1,0:T(8,128)(2,1)S(1)}, bf16[256,1152]{1,0:T(8,128)(2,1)S(1)}, u32[]{:S(2)}, u32[]{:S(2)}) %collective-permute-start.9) | collective-permute-done | bytes 589856 | tf_op jit(solution)/shard_map/ppermute | solution.py:381
  126.1 2.6 %close.1 = (f32[1024,128]{1,0:T(8,128)}, f32[1024,128]{1,0:T(8,128)}, f32[128,128]{1,0:T(8,128)}, f32[128,128]{1,0:T(8,128)}) custom-call(f32[2,256,1152]{2,1,0:T(8,128)S(1)} %get-tuple-element.69.own, f32[256,1152]{1,0:T(8,128)} %collective-permute-done.8.core, bf16[256,1152]{1,0:T(8,128)(2,1)S(1)} %collective-permute-done.9.chip), custom_call_target="tpu_custom_call" | custom-call | tf_op jit(solution)/shard_map/close/pallas_call | solution.py:318
  128.6 2.1 %finish.1 = bf16[16,8192]{1,0:T(8,128)(2,1)} custom-call(bf16[32,128,128]{2,1,0:T(8,128)(2,1)} %all-to-all-done.1.parts), custom_call_target="tpu_custom_call" | custom-call | tf_op jit(solution)/shard_map/finish/pallas_call | solution.py:295
  (32 shorter events, 2.2 us)
Async XLA Ops:
  0.6 12.0 %copy-start.3 = (f32[128,8]{0,1:T(8,128)S(1)}, f32[128,8]{0,1:T(8,128)}, u32[]{:S(2)}) copy-start(f32[128,8]{0,1:T(8,128)} %param.14) | copy-start | bytes 12292
  0.6 33.8 %copy-start.1 = (s32[8]{0:T(128)S(1)}, s32[8]{0:T(128)}, u32[]{:S(2)}) copy-start(s32[8]{0:T(128)} %refs_1_.11) | copy-start | bytes 100
  4.1 17.9 %collective-permute-start.2 = (bf16[2304,128]{1,0:T(8,128)(2,1)S(1)}, bf16[2304,128]{1,0:T(8,128)(2,1)}, u32[]{:S(2)}, u32[]{:S(2)}) collective-permute-start(bf16[2304,128]{1,0:T(8,128)(2,1)S(1)} %join.1.refs_3_.refs_5_), channel_id=1, source_target_pairs={{0,16},{16,0},{1,17},{17,1},{2,18},{18,2},{3,19},{19,3},{4,20},{20... | collective-permute-start | bytes 1769480 | tf_op jit(solution)/shard_map/ppermute | solution.py:360
  7.3 23.2 %all-to-all-start = ((bf16[8,272,128]{2,1,0:T(8,128)(2,1)}), bf16[8,272,128]{2,1,0:T(8,128)(2,1)}, u32[]{:S(2)}, u32[]{:S(2)}) async-start(bf16[8,272,128]{2,1,0:T(8,128)(2,1)} %pack.1), calls=%async_computation | async-start | bytes 1114112 | tf_op jit(solution)/shard_map/all_to_all | solution.py:358
  12.6 21.8 %collective-permute-start.4 = (bf16[2304,128]{1,0:T(8,128)(2,1)S(1)}, bf16[2304,128]{1,0:T(8,128)(2,1)S(1)}, u32[]{:S(2)}, u32[]{:S(2)}) collective-permute-start(bf16[2304,128]{1,0:T(8,128)(2,1)S(1)} %join.1.refs_3_.refs_5_), channel_id=1, source_target_pairs={{0,8},{8,0},{1,9},{9,1},{2,10},{10,2},{3,11},{11,3},{4,12},{12,4},... | collective-permute-start | bytes 1769480 | tf_op jit(solution)/shard_map/ppermute | solution.py:361
  22.0 19.7 %collective-permute-start.3 = (bf16[2304,128]{1,0:T(8,128)(2,1)}, bf16[2304,128]{1,0:T(8,128)(2,1)}, u32[]{:S(2)}, u32[]{:S(2)}) collective-permute-start(bf16[2304,128]{1,0:T(8,128)(2,1)} %collective-permute-done.2.refs_3_.refs_4_), channel_id=1, source_target_pairs={{0,8},{8,0},{1,9},{9,1},{2,10},{10,2},{3,11},{11,3},{4,12},{12,4},... | collective-permute-start | bytes 1769480 | tf_op jit(solution)/shard_map/ppermute | solution.py:362
  31.2 17.4 %collective-permute-start.1 = (bf16[8,272,128]{2,1,0:T(8,128)(2,1)}, bf16[8,272,128]{2,1,0:T(8,128)(2,1)}, u32[]{:S(2)}, u32[]{:S(2)}) collective-permute-start(bf16[8,272,128]{2,1,0:T(8,128)(2,1)} %maximum_dynamic-update-slice_fusion.refs_2_), channel_id=1, source_target_pairs={{0,32},{32,64},{64,96},{96,0},{1,33},{33,65},{65,97},{97,1},{2,34}... | collective-permute-start | bytes 1671176 | tf_op jit(solution)/shard_map/ppermute | solution.py:365
  32.7 15.8 %collective-permute-start = (bf16[8,272,128]{2,1,0:T(8,128)(2,1)}, bf16[8,272,128]{2,1,0:T(8,128)(2,1)}, u32[]{:S(2)}, u32[]{:S(2)}) collective-permute-start(bf16[8,272,128]{2,1,0:T(8,128)(2,1)} %maximum_dynamic-update-slice_fusion.refs_2_), channel_id=1, source_target_pairs={{0,96},{32,0},{64,32},{96,64},{1,97},{33,1},{65,33},{97,65},{2,98}... | collective-permute-start | bytes 1671176 | tf_op jit(solution)/shard_map/ppermute | solution.py:364
  50.5 15.2 %collective-permute-start.5 = (bf16[4,272,128]{2,1,0:T(8,128)(2,1)S(1)}, bf16[4,272,128]{2,1,0:T(8,128)(2,1)S(1)}, u32[]{:S(2)}, u32[]{:S(2)}) collective-permute-start(bf16[4,272,128]{2,1,0:T(8,128)(2,1)S(1)} %slice.37), channel_id=1, source_target_pairs={{0,96},{32,0},{64,32},{96,64},{1,97},{33,1},{65,33},{97,65},{2,98}... | collective-permute-start | bytes 835592 | tf_op jit(solution)/shard_map/ppermute | solution.py:374
  52.4 13.4 %collective-permute-start.6 = (bf16[4,272,128]{2,1,0:T(8,128)(2,1)S(1)}, bf16[4,272,128]{2,1,0:T(8,128)(2,1)S(1)}, u32[]{:S(2)}, u32[]{:S(2)}) collective-permute-start(bf16[4,272,128]{2,1,0:T(8,128)(2,1)S(1)} %slice.38), channel_id=1, source_target_pairs={{0,32},{32,64},{64,96},{96,0},{1,33},{33,65},{65,97},{97,1},{2,34}... | collective-permute-start | bytes 835592 | tf_op jit(solution)/shard_map/ppermute | solution.py:374
  72.5 6.8 %collective-permute-start.7 = (f32[256,1152]{1,0:T(8,128)S(1)}, f32[256,1152]{1,0:T(8,128)S(1)}, u32[]{:S(2)}, u32[]{:S(2)}) collective-permute-start(f32[256,1152]{1,0:T(8,128)S(1)} %slice_bitcast_fusion.1), channel_id=1, source_target_pairs={{0,8},{8,0},{1,9},{9,1},{2,10},{10,2},{3,11},{11,3},{4,12},{12,4},... | collective-permute-start | bytes 3538952 | tf_op jit(solution)/shard_map/ppermute | solution.py:378
  92.2 1.6 %copy-start = (bf16[4,8,128,128]{3,2,1,0:T(8,128)(2,1)}, bf16[4,8,128,128]{3,2,1,0:T(8,128)(2,1)S(1)}, u32[]{:S(2)}) copy-start(bf16[4,8,128,128]{3,2,1,0:T(8,128)(2,1)S(1)} %get-tuple-element.68) | copy-start | bytes 3145732
  92.2 6.5 %copy-start.2 = (bf16[256,1152]{1,0:T(8,128)(2,1)S(1)}, bf16[256,1152]{1,0:T(8,128)(2,1)}, u32[]{:S(2)}) copy-start(bf16[256,1152]{1,0:T(8,128)(2,1)} %fusion) | copy-start | bytes 1769476
  93.3 32.7 %collective-permute-start.8 = (f32[256,1152]{1,0:T(8,128)}, f32[256,1152]{1,0:T(8,128)}, u32[]{:S(2)}, u32[]{:S(2)}) collective-permute-start(f32[256,1152]{1,0:T(8,128)} %slice_bitcast_fusion), channel_id=1, source_target_pairs={{0,8},{8,0},{1,9},{9,1},{2,10},{10,2},{3,11},{11,3},{4,12},{12,4},... | collective-permute-start | bytes 3538952 | tf_op jit(solution)/shard_map/ppermute | solution.py:386
  93.8 34.8 %all-to-all-start.1 = ((bf16[32,128,128]{2,1,0:T(8,128)(2,1)}), bf16[32,128,128]{2,1,0:T(8,128)(2,1)}, u32[]{:S(2)}, u32[]{:S(2)}) async-start(bf16[32,128,128]{2,1,0:T(8,128)(2,1)} %bitcast.17), calls=%async_computation.1 | async-start | bytes 2097152 | tf_op jit(solution)/shard_map/all_to_all | solution.py:387
  98.7 27.3 %collective-permute-start.9 = (bf16[256,1152]{1,0:T(8,128)(2,1)S(1)}, bf16[256,1152]{1,0:T(8,128)(2,1)S(1)}, u32[]{:S(2)}, u32[]{:S(2)}) collective-permute-start(bf16[256,1152]{1,0:T(8,128)(2,1)S(1)} %copy-done.2), channel_id=1, source_target_pairs={{0,16},{16,0},{1,17},{17,1},{2,18},{18,2},{3,19},{19,3},{4,20},{20... | collective-permute-start | bytes 1769480 | tf_op jit(solution)/shard_map/ppermute | solution.py:381
